TPU v7x, 32 devices: a whole 2x2x4 slice. The times are simulated.
32 devices in a mesh: row: 4 (over z), col: 4 (over y, x), freq: 2 (over core).
Axes of the slice: x: 2, y: 2, z: 4, core: 2. Of those that a mesh axis runs over, the one named last changes fastest.
Arguments:
- spectra: bfloat16 [10240, 4096], P(('row', 'col'), 'freq'), parts along dimension 1, may hold values from -6 to 6
- loading: float32 [20480], P('freq'), parts along dimension 0, may hold values from 0.05 to 0.5
- delays: int32 [10240, 512], P('row', 'col'), may hold values from 0 to 1023
- bin_index: int32 [2], P('freq'), parts along dimension 0, may hold values from 1 to 1023
Outputs:
- trailing: float32 [20480, 10240], P(('freq', 'row'), 'col'), parts along dimension 0
- panel: float32 [20480, 512], P(('freq', 'row')), parts along dimension 0
- whitened: float32 [2, 20480, 512], P(None, ('freq', 'row'), 'col'), parts along dimension 1
There are 2 independent parts, one for each index of `freq`. A program takes and returns all parts, laid end to end along the dimension named above; an argument that names none is the same for every part. Nothing has to cross between parts.
All inputs are finite; a program needn't handle non-finite values.
Results may differ from a plain program's by a relative error of at most 0.0003.
Values may be sent and summed in bfloat16 or wider, within the bound.
No kernel may reach another device: no remote copies, remote signals or barrier semaphores. Data moves between devices by JAX's collectives and lax.ppermute only.
A program may use at most 192 MiB of HBM per device.

v0:
```python
import jax
import jax.numpy as jnp
from jax import lax
from jax.sharding import PartitionSpec as P

PANEL = 512
NFFT = 2048


two_pi = 6.283185307179586


def from_root(value, axis, source):
    kept = jnp.where(lax.axis_index(axis) == source, value, 0).astype(value.dtype)
    return lax.psum(kept, axis)


def lower_solve(factor, right_side):
    return jax.scipy.linalg.solve_triangular(factor, right_side, lower=True)


def gram_head(source, loading, snap_count):
    head_csd = jnp.dot(source, source.T, preferred_element_type=jnp.float32) / snap_count
    return jnp.linalg.cholesky(head_csd + jnp.diag(loading[:PANEL]))


def on_device(spectra, loading, delays, bin_index):
    row_index = lax.axis_index("row")
    col_index = lax.axis_index("col")
    tile_size = delays.shape[0]
    slow_count = delays.shape[1]
    snap_count = spectra.shape[1] // 2
    own_rows = lax.all_gather(spectra, "col", axis=0, tiled=True)
    col_rows = from_root(own_rows, "row", col_index)
    row_load = lax.dynamic_slice_in_dim(loading, row_index * tile_size, tile_size)
    tile_csd = jnp.dot(own_rows, col_rows.T, preferred_element_type=jnp.float32) / snap_count
    tile_csd = tile_csd + jnp.where(row_index == col_index, jnp.diag(row_load), 0.0)
    head_rows = from_root(own_rows[:PANEL], "row", 0)
    factor = gram_head(head_rows, loading, snap_count)
    head_load = jnp.eye(tile_size, PANEL, dtype=jnp.float32) * loading[:PANEL][None, :]
    own_side = jnp.dot(own_rows, head_rows.T, preferred_element_type=jnp.float32) / snap_count
    own_side = own_side + jnp.where(row_index == 0, head_load, 0.0)
    col_side = jnp.dot(col_rows, head_rows.T, preferred_element_type=jnp.float32) / snap_count
    col_side = col_side + jnp.where(col_index == 0, head_load, 0.0)
    own_panel = lower_solve(factor, own_side.T).T
    col_panel = lower_solve(factor, col_side.T).T
    glob_rows = row_index * tile_size + jnp.arange(tile_size)
    glob_cols = col_index * tile_size + jnp.arange(tile_size)
    update = tile_csd - jnp.dot(
        own_panel, col_panel.T, precision=lax.Precision.HIGHEST, preferred_element_type=jnp.float32
    )
    keep_mask = (glob_rows[:, None] >= PANEL) & (glob_cols[None, :] >= PANEL)
    trailing = jnp.where(keep_mask, update, 0.0)
    phase_int = delays * bin_index[0] % NFFT
    phase_angle = phase_int.astype(jnp.float32) * (two_pi / NFFT)
    steer_tile = jnp.concatenate([jnp.cos(phase_angle), jnp.sin(phase_angle)], axis=1)
    solved = lower_solve(factor, steer_tile[:PANEL])
    solved = from_root(solved, "row", 0)
    lower_rows = steer_tile - jnp.dot(
        own_panel, solved, precision=lax.Precision.HIGHEST, preferred_element_type=jnp.float32
    )
    padded = jnp.pad(solved, ((0, tile_size - PANEL), (0, 0)))
    stacked = jnp.where(glob_rows[:, None] < PANEL, padded, lower_rows)
    whitened = jnp.stack([stacked[:, :slow_count], stacked[:, slow_count:]])
    return (trailing, own_panel, whitened)


def solution(mesh):
    return jax.shard_map(
        on_device,
        mesh=mesh,
        in_specs=(P(("row", "col"), "freq"), P("freq"), P("row", "col"), P("freq")),
        out_specs=(
            P(("freq", "row"), "col"),
            P(("freq", "row"), None),
            P(None, ("freq", "row"), "col"),
        ),
        check_vma=False,
    )
```

profile of v0, /device:TPU:0, one launch (start us, length us, event | category | flops | bytes accessed | tf_op | source)
XLA Modules:
  0.0 915.4 jit_solution(6345057209620928680)
XLA Ops:
  7.2 0.7 all-gather.2.cloned.1.call-update
  8.0 109.7 %all-gather.2.cloned.1.call-done = bf16[2560,2048]{1,0:T(8,128)(2,1)} async-done(((bf16[640,2048]{1,0:T(8,128)(2,1)}), bf16[2560,2048]{1,0:T(8,128)(2,1)}) %all-gather.2.cloned.1.call-update) | async-done | bytes 10485776 | tf_op jit(solution)/shard_map/all_gather | solution.py:33
  117.6 3.0 slice_select_fusion
  120.7 8.7 broadcast_select_fusion
  129.5 0.7 slice.155
  130.2 0.8 dynamic_slice.3
  131.7 7.1 fusion.54
  138.8 417.6 %all-reduce.8.cloned.1.call-done = (bf16[512,2048]{1,0:T(8,128)(2,1)}, bf16[2560,2048]{1,0:T(8,128)(2,1)}) async-done(((bf16[512,2048]{1,0:T(8,128)(2,1)}, bf16[2560,2048]{1,0:T(8,128)(2,1)}), (bf16[512,2048]{1,0:T(8,128)(2,1)}, bf16[2560,2048]{1,0:T(8,128)(2,1)})) %all-reduce.8.cloned.1.call-update) | async-done | bytes 12582928 | tf_op jit(solution)/shard_map/psum | solution.py:15
  556.4 4.5 convolution_multiply_fusion
  560.9 2.5 copy.7
  563.4 1.8 add_multiply_fusion
  565.2 1.0 copy-done.7
  566.2 11.7 %cholesky.103 = f32[128,128]{1,0:T(8,128)S(1)} custom-call(f32[128,128]{1,0:T(8,128)S(1)} %cholesky.263), custom_call_target="Cholesky" | custom-call | tf_op jit(solution)/shard_map/jit(cholesky)/cholesky | solution.py:24
  577.9 1.1 cholesky.222
  579.0 9.8 %custom-call.34 = f32[1,128,128]{1,2,0:T(8,128)S(1)} custom-call(f32[1,128,128]{2,1,0:T(8,128)S(1)} %get-tuple-element.56), custom_call_target="InvertDiagBlocksLowerTriangular" | custom-call | tf_op jit(solution)/shard_map/jit(cholesky)/cholesky | solution.py:24
  588.8 1.9 constant_dynamic-update-slice_fusion.3
  590.7 1.2 convolution_subtract_fusion.5
  592.0 11.7 %cholesky.215 = f32[128,128]{1,0:T(8,128)S(1)} custom-call(f32[128,128]{1,0:T(8,128)S(1)} %cholesky.267), custom_call_target="Cholesky" | custom-call | tf_op jit(solution)/shard_map/jit(cholesky)/cholesky | solution.py:24
  603.7 0.6 select_reduce_fusion.2
  604.4 9.8 %custom-call.35 = f32[1,128,128]{1,2,0:T(8,128)S(1)} custom-call(f32[1,128,128]{2,1,0:T(8,128)S(1)} %get-tuple-element.53), custom_call_target="InvertDiagBlocksLowerTriangular" | custom-call | tf_op jit(solution)/shard_map/jit(cholesky)/cholesky | solution.py:24
  614.2 0.9 convolution_dynamic-update-slice_fusion
  615.1 1.4 convolution_subtract_fusion.8
  616.5 11.7 %cholesky.236 = f32[128,128]{1,0:T(8,128)S(1)} custom-call(f32[128,128]{1,0:T(8,128)S(1)} %cholesky.272), custom_call_target="Cholesky" | custom-call | tf_op jit(solution)/shard_map/jit(cholesky)/cholesky | solution.py:24
  628.3 0.6 select_reduce_fusion.1
  628.9 9.8 %custom-call.36 = f32[1,128,128]{1,2,0:T(8,128)S(1)} custom-call(f32[1,128,128]{2,1,0:T(8,128)S(1)} %get-tuple-element.50), custom_call_target="InvertDiagBlocksLowerTriangular" | custom-call | tf_op jit(solution)/shard_map/jit(cholesky)/cholesky | solution.py:24
  638.7 0.8 convolution_dynamic-update-slice_fusion.1
  639.5 1.4 convolution_subtract_fusion.10
  641.0 24.1 %cholesky.253 = f32[128,128]{1,0:T(8,128)S(1)} custom-call(f32[128,128]{1,0:T(8,128)S(1)} %convolution_subtract_fusion.10), custom_call_target="Cholesky" | custom-call | tf_op jit(solution)/shard_map/jit(cholesky)/cholesky | solution.py:24
  665.1 0.6 select_reduce_fusion
  665.7 0.7 compare_reduce_fusion.1
  666.4 0.7 compare_reduce_fusion
  667.1 0.6 compare_reduce_fusion.2
  670.3 2.3 select_select_fusion.2
  672.6 11.6 %while.5 = (s32[]{:T(128)}, f32[512,512]{1,0:T(8,128)}, s32[4,2]{0,1:T(2,128)S(1)}, f32[4,128,128]{2,1,0:T(8,128)S(1)}, s32[]{:T(128)}) while((s32[]{:T(128)}, f32[512,512]{1,0:T(8,128)}, s32[4,2]{0,1:T(2,128)S(1)}, f32[4,128,128]{2,1,0:T(8,128)S(1)}, s32[]{:T(128)}) %tuple.43), condition=%wide.while_cond, body=%wide.while_body.sunk | while | flops 2 | bytes 131189 | solution.py:19
  673.2 2.3 bitcast_dynamic-update-slice_fusion.2
  675.6 0.5 fusion.128
  676.1 2.3 bitcast_dynamic-update-slice_fusion.2
  679.0 2.3 bitcast_dynamic-update-slice_fusion.2
  681.9 2.2 bitcast_dynamic-update-slice_fusion.2
  684.2 39.3 %custom-call.39 = f32[4,128,128]{1,2,0:T(8,128)S(1)} custom-call(f32[4,128,128]{2,1,0:T(8,128)S(1)} %get-tuple-element.26), custom_call_target="InvertDiagBlocksLowerTriangular" | custom-call | tf_op jit(solution)/shard_map/jit(_solve_triangular)/triangular_solve | solution.py:19
  723.5 9.3 %fusion.3 = f32[512,2560]{1,0:T(8,128)S(1)} fusion(bf16[512,2048]{1,0:T(8,128)(2,1)} %get-tuple-element.39, bf16[2560,2048]{1,0:T(8,128)(2,1)} %get-tuple-element.40, f32[512]{0:T(512)S(1)} %slice.155, pred[]{:T(512)S(6)} %eq.36), kind=kOutput, calls=%fused_computation.10 | convolution fusion | flops 5375262720 | bytes 17827840 | tf_op jit(solution)/shard_map/dot_general | solution.py:43
  732.8 1.3 fusion.40
  734.1 1.3 convolution_subtract_fusion.1
  735.4 1.3 fusion.79
  736.7 1.5 convolution_subtract_fusion.3
  738.2 1.3 fusion.82
  739.5 2.5 fusion.25
  742.0 2.3 fusion.85
  744.3 6.0 fusion.2
  750.4 1.3 fusion.42
  751.6 1.3 convolution_subtract_fusion.2
  752.9 1.3 fusion.80
  754.2 1.5 convolution_subtract_fusion.4
  755.7 1.3 fusion.83
  757.0 2.5 fusion.28
  759.5 2.5 fusion.86
  764.3 0.8 maximum_select_fusion
  765.1 48.0 %fusion.4 = f32[2560,2560]{0,1:T(8,128)} fusion(f32[128,2560]{1,0:T(8,128)} %fusion.85, f32[128,2560]{1,0:T(8,128)} %copy-done.6, f32[128,2560]{1,0:T(8,128)} %copy-done.4, f32[128,2560]{1,0:T(8,128)} %copy-done.2, f32[128,2560]{1,0:T(8,128)} %fusion.86, f32[128,2560]{1,0:T(8,128)} %copy-done.3, f32[128,2560]{1,0:T(8,128)} %copy-done.1, f32[128,2560]{1,0:T(8,128)} %copy-done), kind=kOutput, calls=%fused_computation.12 | convolution fusion | flops 40273182720 | bytes 36700160 | tf_op jit(solution)/shard_map/dot_general | solution.py:49
  813.1 43.3 %fusion.1 = f32[2560,2560]{0,1:T(8,128)} fusion(f32[2560,2560]{0,1:T(8,128)} %fusion.4, bf16[2560,2048]{1,0:T(8,128)(2,1)} %get-tuple-element.40, bf16[2560,2048]{1,0:T(8,128)(2,1)} %all-gather.2.cloned.1.call-done, f32[2560]{0:T(1024)S(1)} %dynamic_slice.3, pred[]{:T(512)S(6)} %eq.30, pred[2560]{0:T(1024)(128)(4,1)S(1)} %get-tuple-element.62, ...), kind=kOutput, calls=%fused_computation.4 | convolution fusion | flops 26895974400 | bytes 73415680 | tf_op jit(solution)/shard_map/dot_general | solution.py:36
  856.4 27.3 %copy.9 = f32[2560,2560]{1,0:T(8,128)} copy(f32[2560,2560]{0,1:T(8,128)} %fusion.1) | data formatting | bytes 52428800
  883.7 4.2 fusion.44
  887.9 5.9 copy.10
  893.8 12.8 %fusion.12 = f32[2560,256]{1,0:T(8,128)S(1)} fusion(f32[512,256]{1,0:T(8,128)} %all-reduce.6.cloned.1.call-done, f32[2560,128]{1,0:T(8,128)S(1)} %get-tuple-element.45, f32[2560,128]{1,0:T(8,128)S(1)} %get-tuple-element.46, pred[2560]{0:T(1024)(128)(4,1)S(1)} %get-tuple-element.61, f32[128,2560]{1,0:T(8,128)} %fusion.86, f32[128,2560]{1,0:T(8,128)} %copy-done.3, ...), kind=kOutput, calls=%fused_computation.31 | convolution fusion | flops 4032430080 | bytes 11012608 | tf_op jit(solution)/shard_map/dot_general | solution.py:59
  906.8 1.7 pad_maximum_fusion.2
  (54 shorter events, 4.5 us)
Async XLA Ops:
  7.2 110.5 %all-gather.2.cloned.1.call-start = ((), (), s32[]{:S(2)}) async-start(), calls=%async_computation | async-start | bytes 13107200 | tf_op jit(solution)/shard_map/all_gather | solution.py:33
  7.9 548.5 %all-reduce.8.cloned.1.call-start = ((), (), s32[]{:S(2)}) async-start(), calls=%async_computation.2 | async-start | bytes 25165824 | tf_op jit(solution)/shard_map/psum | solution.py:15
  129.4 764.3 %all-reduce.6.cloned.1.call-start = ((), (), s32[]{:S(2)}) async-start(), calls=%async_computation.1 | async-start | bytes 1048576 | tf_op jit(solution)/shard_map/psum | solution.py:15
  565.2 1.0 copy-start.7
  732.8 1.3 copy-start.5
  734.1 5.3 copy-start.2
  735.4 9.0 slice-start
  736.6 2.8 copy-start.4
  736.6 7.7 slice-start.1
  739.5 2.5 copy-start.6
  739.5 4.9 slice-start.2
  742.0 2.3 copy-start.8
  751.6 5.3 copy-start
  754.2 2.8 copy-start.1
  757.0 2.5 copy-start.3
Sparse Core Ops, SparseCore 0:
  9.8 107.7 all-gather.1
  129.6 426.7 all-reduce.7
  765.2 37.1 all-reduce.5
where the time goes:
time: 927 us; the launch traced here: 915 us
  waiting for transfers between devices  528 us (57%)
  other arithmetic  162 us (17%)
  matrix products  157 us (17%)
  local copies, waits for them, and re-layouts  51 us (6%)
  between operations  17.9 us (2%)
    psum x2, waiting for transfers between devices, from_root(): return lax.psum(kept, axis)  418 us
    all_gather x1, waiting for transfers between devices, on_device(): own_rows = lax.all_gather(spectra, 'col', axis=0, tiled=True)  110 us
    another operation x14, other arithmetic, gram_head(): return jnp.linalg.cholesky(head_csd + jnp.diag(loading[:PANEL]))  92.6 us
    dot_general x1, matrix products, on_device(): jnp.dot(own_panel, col_panel.T, precision=lax.Precision.HIGHEST, preferre...  48 us
    dot_general x1, matrix products, on_device(): jnp.dot(own_rows, col_rows.T, preferred_element_type=jnp.float32)  43.3 us
    another operation x4, other arithmetic, lower_solve(): return jax.scipy.linalg.solve_triangular(factor, right_side, lower=True)  41.7 us
    unnamed x26, local copies, waits for them, and re-layouts  34.2 us
    another operation x21, matrix products, lower_solve(): return jax.scipy.linalg.solve_triangular(factor, right_side, lower=True)  25.1 us
  transfers between devices with their start and end apart: 3, of which 2 were waited for; matrix products, arithmetic and copies ran while one was open for 15% of the time, Pallas kernels for 0%

commit v1 on v0

v1 whole, which is shorter than its diff:
```python
import functools

import jax
import jax.numpy as jnp
from jax import lax
from jax.experimental import pallas as pl
from jax.experimental.pallas import tpu as pltpu
from jax.sharding import PartitionSpec as P

PANEL = 512
NFFT = 2048
BLK = 128
SUB = 8

two_pi = 6.283185307179586
F32 = jnp.float32
BF16 = jnp.bfloat16
HIGHEST = lax.Precision.HIGHEST
NT = (((1,), (1,)), ((), ()))


def dot_nt(a, b, precision=None):
    return lax.dot_general(a, b, NT, precision=precision, preferred_element_type=F32)


def split(x):
    high = x.astype(BF16)
    return high, (x - high.astype(F32)).astype(BF16)


def vmem(shape=None, index=None):
    if shape is None:
        return pl.BlockSpec(memory_space=pltpu.VMEM)
    return pl.BlockSpec(shape, index, memory_space=pltpu.VMEM)


SMEM = pl.BlockSpec(memory_space=pltpu.SMEM)
ANY = pl.BlockSpec(memory_space=pl.ANY)


def cost(flops, nbytes):
    return pl.CostEstimate(flops=int(flops), bytes_accessed=int(nbytes), transcendentals=0)


def lanes_of(x, j):
    return jnp.broadcast_to(x[:, j : j + 1], x.shape)


def rows_of(x, i):
    return jnp.broadcast_to(x[i : i + 1], x.shape)


def inverse_factor(block):
    n = block.shape[0]
    sub = lax.broadcasted_iota(jnp.int32, (SUB, n), 0)
    diagonal = lax.broadcasted_iota(jnp.int32, (n, n), 0) == lax.broadcasted_iota(jnp.int32, (n, n), 1)
    left = block
    right = jnp.where(diagonal, 1.0, 0.0).astype(F32)
    done = []
    for v in range(n // SUB):
        top, inv = left[:SUB], right[:SUB]
        columns = [lanes_of(top, SUB * v + k) for k in range(SUB)]
        for j in range(SUB):
            scale = lax.rsqrt(rows_of(columns[j], j))
            coef = columns[j] * scale
            for k in range(j + 1, SUB):
                columns[k] = columns[k] - coef * rows_of(coef, k)
            own_top, own_inv = rows_of(top, j) * scale, rows_of(inv, j) * scale
            top = jnp.where(sub == j, own_top, jnp.where(sub > j, top - coef * own_top, top))
            inv = jnp.where(sub == j, own_inv, jnp.where(sub > j, inv - coef * own_inv, inv))
        done.append(inv)
        if SUB * (v + 1) < n:
            below = jnp.transpose(top)[SUB * (v + 1) :, :]
            left = left[SUB:] - jnp.dot(below, top, precision=HIGHEST, preferred_element_type=F32)
            right = right[SUB:] - jnp.dot(below, inv, precision=HIGHEST, preferred_element_type=F32)
    return jnp.concatenate(done, axis=0)


def factor_kernel(snap, parts, spot_ref, *refs):
    pieces, (load_ref, inv_ref, head_ref, csd) = refs[:parts], refs[parts:]
    n = csd.shape[0]
    rows = n // parts
    for m, piece in enumerate(pieces):
        at = pl.multiple_of(jnp.bitwise_xor(spot_ref[0], m) * rows, rows)
        head_ref[pl.ds(at, rows), :] = piece[...]
    row = lax.broadcasted_iota(jnp.int32, (n, n), 0)
    col = lax.broadcasted_iota(jnp.int32, (n, n), 1)
    gram = dot_nt(head_ref[...], head_ref[...]) / snap
    csd[...] = gram + jnp.where(row == col, load_ref[...], 0.0)
    inv_ref[...] = jnp.where(row == col, 1.0, 0.0)
    below = lax.broadcasted_iota(jnp.int32, (n, BLK), 0)

    def step(k, _):
        at = pl.multiple_of(k * BLK, BLK)
        inv = inverse_factor(csd[pl.ds(at, BLK), pl.ds(at, BLK)])
        side = dot_nt(csd[:, pl.ds(at, BLK)], inv, HIGHEST)
        side = jnp.where(below >= at + BLK, side, 0.0)
        own = jnp.dot(inv, inv_ref[pl.ds(at, BLK), :], precision=HIGHEST, preferred_element_type=F32)
        inv_ref[pl.ds(at, BLK), :] = own
        inv_ref[...] -= jnp.dot(side, own, precision=HIGHEST, preferred_element_type=F32)
        csd[...] -= dot_nt(side, side, HIGHEST)
        return 0

    lax.fori_loop(0, n // BLK, step, 0)


def head_factor(spot, pieces, load, snap):
    depth = pieces[0].shape[1]
    n = load.shape[1]
    return pl.pallas_call(
        functools.partial(factor_kernel, snap, len(pieces)),
        out_shape=(jax.ShapeDtypeStruct((n, n), F32), jax.ShapeDtypeStruct((n, depth), BF16)),
        in_specs=[SMEM] + [vmem()] * (len(pieces) + 1),
        out_specs=(vmem(), vmem()),
        scratch_shapes=[pltpu.VMEM((n, n), F32)],
        compiler_params=pltpu.CompilerParams(vmem_limit_bytes=40 << 20),
        cost_estimate=cost(40e9, 4e6),
    )(spot, *pieces, load)


def panel_kernel(snap, spot_ref, rows_ref, head_ref, inv_ref, load_ref, panel_ref, high_ref, low_ref):
    side = dot_nt(rows_ref[...], head_ref[...]) / snap
    row = lax.broadcasted_iota(jnp.int32, side.shape, 0) + (spot_ref[0] + pl.program_id(0) * side.shape[0])
    side = side + jnp.where(row == lax.broadcasted_iota(jnp.int32, side.shape, 1), load_ref[...], 0.0)
    panel = dot_nt(side, inv_ref[...], HIGHEST)
    panel_ref[...] = panel
    high, low = split(panel)
    high_ref[...] = high
    low_ref[...] = low


def own_panel(first, rows, head, inv, load, snap, tile):
    n, depth = rows.shape
    width = head.shape[0]
    return pl.pallas_call(
        functools.partial(panel_kernel, snap),
        grid=(n // tile,),
        out_shape=tuple(jax.ShapeDtypeStruct((n, width), t) for t in (F32, BF16, BF16)),
        in_specs=[
            SMEM,
            vmem((tile, depth), lambda i: (i, 0)),
            vmem((width, depth), lambda i: (0, 0)),
            vmem((width, width), lambda i: (0, 0)),
            vmem((1, width), lambda i: (0, 0)),
        ],
        out_specs=tuple(vmem((tile, width), lambda i: (i, 0)) for _ in range(3)),
        compiler_params=pltpu.CompilerParams(vmem_limit_bytes=40 << 20),
        cost_estimate=cost(2 * n * width * (depth + 6 * width), 2 * n * depth + 8 * n * width),
    )(first, rows, head, inv, load)


def trailing_kernel(snap, geo, gather, spot_ref, *refs):
    tile, groups, width, stride, first, size = geo
    parts = 7 if gather else 1
    sources = refs[:parts]
    rows_ref, high_ref, low_ref, head_ref, inv_ref, load_ref = refs[parts : parts + 6]
    out_ref, cols_ref, col_high, col_low, acc, out_sem, in_sem = refs[len(refs) - 7 :]
    row_at, col_at = spot_ref[0], spot_ref[1]
    step, steps = pl.program_id(0), pl.num_programs(0)
    slot = lax.rem(step, 2)

    def out_copies(slot, step):
        at = pl.multiple_of(step * tile, tile)
        return [
            pltpu.make_async_copy(
                acc.at[slot, :, pl.ds(g * width, width)],
                out_ref.at[pl.ds(at, tile), pl.ds(g * stride + first, width)],
                out_sem.at[slot],
            )
            for g in range(groups)
        ]

    @pl.when(step == 0)
    def _():
        if gather:
            own, ups, downs = sources[0], sources[1:4], sources[4:7]
            piece = width // 4

            def pull(src, plane):
                for g in range(groups):
                    pltpu.make_async_copy(
                        src.at[pl.ds(g * piece, piece)],
                        cols_ref.at[pl.ds(pl.multiple_of(g * width + plane * piece, piece), piece)],
                        in_sem,
                    ).start()

            pull(own, row_at)
            for j in range(1, 4):

                @pl.when(row_at >= j)
                def _(j=j):
                    pull(ups[j - 1], row_at - j)

                @pl.when(row_at < j)
                def _(j=j):
                    pull(downs[3 - j], row_at - j + 4)

        else:
            pltpu.make_async_copy(sources[0], cols_ref, in_sem).start()
        pltpu.make_async_copy(cols_ref, cols_ref, in_sem).wait()
        side = dot_nt(cols_ref[...], head_ref[...]) / snap
        high, low = split(dot_nt(side, inv_ref[...], HIGHEST))
        col_high[...] = high
        col_low[...] = low

    @pl.when(step >= 2)
    def _():
        pltpu.make_async_copy(acc.at[slot], acc.at[slot], out_sem.at[slot]).wait()

    total = dot_nt(rows_ref[...], cols_ref[...]) / snap
    total -= dot_nt(high_ref[...], col_high[...])
    total -= dot_nt(high_ref[...], col_low[...])
    total -= dot_nt(low_ref[...], col_high[...])
    row = lax.broadcasted_iota(jnp.int32, (tile, width), 0) + (row_at * size + step * tile)
    for g in range(groups):
        col = lax.broadcasted_iota(jnp.int32, (tile, width), 1) + (col_at * size + g * stride + first)
        load = load_ref[0:1, g * stride + first : g * stride + first + width]
        mine = total[:, g * width : (g + 1) * width] + jnp.where(row == col, load, 0.0)
        acc[slot, :, g * width : (g + 1) * width] = jnp.where((row >= PANEL) & (col >= PANEL), mine, 0.0)
    for copy in out_copies(slot, step):
        copy.start()

    @pl.when(step == steps - 1)
    def _():
        for k in range(2):
            pltpu.make_async_copy(acc.at[k], acc.at[k], out_sem.at[k]).wait()


def trailing_part(spot, sources, rows, high, low, head, inv, load, so_far, snap, geo):
    tile, groups, width, stride, first, size = geo
    n, depth = rows.shape
    panel = head.shape[0]
    count = groups * width
    gather = len(sources) > 1
    given = [spot, *sources, rows, high, low, head, inv, load]
    specs = [SMEM] + [ANY] * len(sources) + [
        vmem((tile, depth), lambda i: (i, 0)),
        vmem((tile, panel), lambda i: (i, 0)),
        vmem((tile, panel), lambda i: (i, 0)),
        vmem((panel, depth), lambda i: (0, 0)),
        vmem((panel, panel), lambda i: (0, 0)),
        vmem((1, size), lambda i: (0, 0)),
    ]
    alias = {}
    if so_far is not None:
        alias = {len(given): 0}
        given.append(so_far)
        specs.append(ANY)
    return pl.pallas_call(
        functools.partial(trailing_kernel, snap, geo, gather),
        grid=(n // tile,),
        out_shape=jax.ShapeDtypeStruct((n, size), F32),
        in_specs=specs,
        out_specs=ANY,
        scratch_shapes=[
            pltpu.VMEM((count, depth), BF16),
            pltpu.VMEM((count, panel), BF16),
            pltpu.VMEM((count, panel), BF16),
            pltpu.VMEM((2, tile, count), F32),
            pltpu.SemaphoreType.DMA((2,)),
            pltpu.SemaphoreType.DMA,
        ],
        input_output_aliases=alias,
        compiler_params=pltpu.CompilerParams(vmem_limit_bytes=56 << 20),
        cost_estimate=cost(2 * n * count * (depth + 3 * panel), 2 * n * depth + 4 * n * count),
    )(*given)


def steer_kernel(spot_ref, steer_ref, top_ref, high_ref, low_ref, inv_ref, out_ref, solved):
    step = pl.program_id(0)
    tile = steer_ref.shape[0]

    @pl.when(step == 0)
    def _():
        solved[...] = jnp.dot(inv_ref[...], top_ref[...], precision=HIGHEST, preferred_element_type=F32)

    s_high, s_low = split(solved[...])
    below = steer_ref[...]
    below -= jnp.dot(high_ref[...], s_high, preferred_element_type=F32)
    below -= jnp.dot(high_ref[...], s_low, preferred_element_type=F32)
    below -= jnp.dot(low_ref[...], s_high, preferred_element_type=F32)
    half = below.shape[1] // 2
    out_ref[0] = below[:, :half]
    out_ref[1] = below[:, half:]

    @pl.when((spot_ref[0] == 0) & (step * tile < PANEL))
    def _():
        mine = solved[pl.ds(pl.multiple_of(step * tile, tile), tile), :]
        out_ref[0] = mine[:, :half]
        out_ref[1] = mine[:, half:]


def whiten(spot, steer, top, high, low, inv, tile):
    n, width = steer.shape
    panel = inv.shape[0]
    return pl.pallas_call(
        steer_kernel,
        grid=(n // tile,),
        out_shape=jax.ShapeDtypeStruct((2, n, width // 2), F32),
        in_specs=[
            SMEM,
            vmem((tile, width), lambda i: (i, 0)),
            vmem((panel, width), lambda i: (0, 0)),
            vmem((tile, panel), lambda i: (i, 0)),
            vmem((tile, panel), lambda i: (i, 0)),
            vmem((panel, panel), lambda i: (0, 0)),
        ],
        out_specs=vmem((2, tile, width // 2), lambda i: (0, i, 0)),
        scratch_shapes=[pltpu.VMEM((panel, width), F32)],
        compiler_params=pltpu.CompilerParams(vmem_limit_bytes=40 << 20),
        cost_estimate=cost(6 * n * panel * width, 8 * n * width + 4 * n * panel),
    )(spot, steer, top, high, low, inv)


def line_kernel(spot_ref, own, *refs):
    ups, downs, out, sem = refs[:3], refs[3:6], refs[6], refs[7]
    n = own.shape[0]
    at = spot_ref[0]

    def put(src, plane):
        pltpu.make_async_copy(src, out.at[pl.ds(pl.multiple_of(plane * n, n), n)], sem).start()

    put(own, at)
    for j in range(1, 4):

        @pl.when(at >= j)
        def _(j=j):
            put(ups[j - 1], at - j)

        @pl.when(at < j)
        def _(j=j):
            put(downs[3 - j], at - j + 4)

    pltpu.make_async_copy(out, out, sem).wait()


def in_line(spot, own, ups, downs):
    n, depth = own.shape
    return pl.pallas_call(
        line_kernel,
        out_shape=jax.ShapeDtypeStruct((4 * n, depth), own.dtype),
        in_specs=[SMEM] + [ANY] * 7,
        out_specs=ANY,
        scratch_shapes=[pltpu.SemaphoreType.DMA],
        cost_estimate=cost(0, 16 * n * depth),
    )(spot, own, *ups, *downs)


def steer_of(delays, bin_index):
    angle = (delays * bin_index % NFFT).astype(F32) * (two_pi / NFFT)
    return jnp.concatenate([jnp.cos(angle), jnp.sin(angle)], axis=1)


def planned(count):
    def move(value, pairs):
        return lax.ppermute(value, ("row", "col"), [(a * count + b, c * count + d) for (a, b), (c, d) in pairs])

    def across(m):
        return [((r, p), (r, p ^ m)) for r in range(count) for p in range(count)]

    def along(k, way):
        planes = [r for r in range(count) if 0 <= r + way < count and 0 <= r - way * (k - 1) < count]
        return [((r, p), (r + way, p)) for r in planes for p in range(count)]

    def line(own):
        ups, downs = [own], [own]
        for k in range(1, count):
            ups.append(move(ups[-1], along(k, 1)))
            downs.append(move(downs[-1], along(k, -1)))
        return ups[1:], downs[1:]

    def chosen(index, values):
        out = values[-1]
        for k in range(len(values) - 2, -1, -1):
            out = jnp.where(index == k, values[k], out)
        return out

    def on_device(spectra, loading, delays, bin_index):
        row, col = lax.axis_index("row"), lax.axis_index("col")
        block, depth = spectra.shape
        size = delays.shape[0]
        snap = depth // 2
        early = block * 3 // 5
        spot_row = row.astype(jnp.int32).reshape(1)
        spot = jnp.stack([row, col]).astype(jnp.int32)

        quarter = PANEL // count
        quarters = [lax.slice_in_dim(spectra, j * quarter, (j + 1) * quarter) for j in range(count)]
        held = chosen(col, [quarters[0]] + [move(quarters[j], [((0, 0), (0, j))]) for j in range(1, count)])
        lifted = [held] + [move(held, [((0, p), (k, p)) for p in range(count)]) for k in range(1, count)]
        piece = chosen(row, lifted)
        pieces = [piece] + [move(piece, across(m)) for m in range(1, count)]

        top = delays[:PANEL].astype(jnp.int16)
        tops = [top] + [move(top, [((0, p), (k, p)) for p in range(count)]) for k in range(1, count)]
        steer_top = steer_of(chosen(row, tops).astype(jnp.int32), bin_index[0])
        steer = steer_of(delays, bin_index[0])

        own_rows = lax.all_gather(spectra, "col", axis=0, tiled=True)

        first = spectra[:early]
        ups, downs = line(first)
        stacked = in_line(spot_row, first, ups, downs)
        cols_first = lax.all_to_all(stacked, "col", 0, 0, tiled=True)
        rest = lax.all_to_all(spectra[early:], "row", 0, 0, tiled=True)
        rest = lax.all_to_all(rest, "col", 0, 0, tiled=True)
        rest_ups, rest_downs = line(rest)

        head_load = loading[:PANEL].reshape(1, PANEL)
        inv, head = head_factor(col.astype(jnp.int32).reshape(1), pieces, head_load, snap)
        panel, high, low = own_panel(spot_row * size, own_rows, head, inv, head_load, snap, size // 10)
        whitened = whiten(spot_row, steer, steer_top, high, low, inv, PANEL // 2)

        load = lax.dynamic_slice_in_dim(loading, col * size, size).reshape(1, size)
        tile = size // 8
        trailing = trailing_part(
            spot, [cols_first], own_rows, high, low, head, inv, load, None, snap,
            (tile, count, early, block, 0, size),
        )
        trailing = trailing_part(
            spot, [rest, *rest_ups, *rest_downs], own_rows, high, low, head, inv, load, trailing, snap,
            (tile, count, block - early, block, early, size),
        )
        return (trailing, panel, whitened)

    return on_device


def from_root(value, axis, source):
    kept = jnp.where(lax.axis_index(axis) == source, value, 0).astype(value.dtype)
    return lax.psum(kept, axis)


def lower_solve(factor, right_side):
    return jax.scipy.linalg.solve_triangular(factor, right_side, lower=True)


def general(spectra, loading, delays, bin_index):
    row_index, col_index = lax.axis_index("row"), lax.axis_index("col")
    size, slow_count = delays.shape
    snap = spectra.shape[1] // 2
    own_rows = lax.all_gather(spectra, "col", axis=0, tiled=True)
    col_rows = from_root(own_rows, "row", col_index)
    row_load = lax.dynamic_slice_in_dim(loading, row_index * size, size)
    tile_csd = jnp.dot(own_rows, col_rows.T, preferred_element_type=F32) / snap
    tile_csd = tile_csd + jnp.where(row_index == col_index, jnp.diag(row_load), 0.0)
    head_rows = from_root(own_rows[:PANEL], "row", 0)
    head_csd = jnp.dot(head_rows, head_rows.T, preferred_element_type=F32) / snap
    factor = jnp.linalg.cholesky(head_csd + jnp.diag(loading[:PANEL]))
    head_load = jnp.eye(size, PANEL, dtype=F32) * loading[:PANEL][None, :]
    own_side = jnp.dot(own_rows, head_rows.T, preferred_element_type=F32) / snap
    own_side = own_side + jnp.where(row_index == 0, head_load, 0.0)
    col_side = jnp.dot(col_rows, head_rows.T, preferred_element_type=F32) / snap
    col_side = col_side + jnp.where(col_index == 0, head_load, 0.0)
    panel = lower_solve(factor, own_side.T).T
    col_panel = lower_solve(factor, col_side.T).T
    glob_rows = row_index * size + jnp.arange(size)
    glob_cols = col_index * size + jnp.arange(size)
    update = tile_csd - jnp.dot(panel, col_panel.T, precision=HIGHEST, preferred_element_type=F32)
    trailing = jnp.where((glob_rows[:, None] >= PANEL) & (glob_cols[None, :] >= PANEL), update, 0.0)
    steer = steer_of(delays, bin_index[0])
    solved = from_root(lower_solve(factor, steer[:PANEL]), "row", 0)
    lower_rows = steer - jnp.dot(panel, solved, precision=HIGHEST, preferred_element_type=F32)
    padded = jnp.pad(solved, ((0, size - PANEL), (0, 0)))
    stacked = jnp.where(glob_rows[:, None] < PANEL, padded, lower_rows)
    whitened = jnp.stack([stacked[:, :slow_count], stacked[:, slow_count:]])
    return (trailing, panel, whitened)


def solution(mesh):
    count = mesh.shape["col"]
    square = mesh.shape["row"] == count
    return jax.shard_map(
        planned(count) if square and count == 4 else general,
        mesh=mesh,
        in_specs=(P(("row", "col"), "freq"), P("freq"), P("row", "col"), P("freq")),
        out_specs=(
            P(("freq", "row"), "col"),
            P(("freq", "row"), None),
            P(None, ("freq", "row"), "col"),
        ),
        check_vma=False,
    )
```

time: 927 us -> 576 us (0.62)
  the two profiles are of different devices: /device:TPU:0 before, /device:TPU:22 now
where the time goes in v1:
time: 576 us; the launch traced here: 575 us
  Pallas kernels  340 us (59%)
  waiting for transfers between devices  121 us (21%)
  starting transfers between devices  66.9 us (12%)
  local copies, waits for them, and re-layouts  16.9 us (3%)
  between operations  15 us (3%)
  other arithmetic  14.8 us (3%)
    pallas_call x1, Pallas kernels, in_line(): pl.pallas_call(line_kernel, out_shape=jax.ShapeDtypeStruct((4 * n, depth)...  192 us
    ppermute x24, waiting for transfers between devices, move(): lax.ppermute(value, ('row', 'col'), [(a * count + b, c * count + d) for (...  113 us
    pallas_call x2, Pallas kernels, trailing_part(): pl.pallas_call(functools.partial(trailing_kernel, snap, geo, gather), gri...  81.2 us
    ppermute x24, starting transfers between devices, move(): lax.ppermute(value, ('row', 'col'), [(a * count + b, c * count + d) for (...  50.6 us
    pallas_call x1, Pallas kernels, head_factor(): pl.pallas_call(functools.partial(factor_kernel, snap, len(pieces)), out_s...  41 us
    pallas_call x1, Pallas kernels, own_panel(): pl.pallas_call(functools.partial(panel_kernel, snap), grid=(n // tile,),...  19.7 us
  transfers between devices with their start and end apart: 28, of which 5 were waited for; matrix products, arithmetic and copies ran while one was open for 4% of the time, Pallas kernels for 53%

profile of v1, /device:TPU:22, one launch (start us, length us, event | category | flops | bytes accessed | tf_op | source)
XLA Modules:
  0.0 575.1 jit_solution(13009107565000518371)
XLA Ops:
  7.2 0.0 all-gather.2.cloned.1.call-start
  7.2 0.7 all-gather.2.cloned.1.call-update
  7.9 1.0 copy-done.10
  8.9 1.2 slice.31.own
  10.1 3.5 collective-permute-start.15
  13.6 2.4 collective-permute-start.18
  16.0 1.0 slice.25
  17.0 6.4 %all-to-all-start = ((bf16[4,64,2048]{2,1,0:T(8,128)(2,1)}), bf16[4,64,2048]{2,1,0:T(8,128)(2,1)}, u32[]{:S(2)}, u32[]{:S(2)}) async-start(bf16[4,64,2048]{2,1,0:T(8,128)(2,1)} %bitcast.13), calls=%async_computation | async-start | bytes 2097152 | tf_op jit(solution)/shard_map/all_to_all | solution.py:405
  23.4 26.2 %collective-permute-done.15.refs_0_ = bf16[384,2048]{1,0:T(8,128)(2,1)} collective-permute-done((bf16[384,2048]{1,0:T(8,128)(2,1)}, bf16[384,2048]{1,0:T(8,128)(2,1)}, u32[]{:S(2)}, u32[]{:S(2)}) %collective-permute-start.15) | collective-permute-done | bytes 1572896 | tf_op jit(solution)/shard_map/ppermute | solution.py:356
  49.6 3.5 collective-permute-start.16
  53.1 0.0 collective-permute-done.18.refs_3_
  53.2 8.0 %collective-permute-start.19 = (bf16[384,2048]{1,0:T(8,128)(2,1)}, bf16[384,2048]{1,0:T(8,128)(2,1)}, u32[]{:S(2)}, u32[]{:S(2)}) collective-permute-start(bf16[384,2048]{1,0:T(8,128)(2,1)} %collective-permute-done.18.refs_3_), channel_id=1, source_target_pairs={{8,0},{10,2},{12,4},{14,6},{16,8},{18,10},{20,12},{22,14},{9,1},{1... | collective-permute-start | bytes 4718600 | tf_op jit(solution)/shard_map/ppermute | solution.py:356
  61.2 1.1 fusion.10
  62.3 1.5 collective-permute-start.6
  63.8 1.5 collective-permute-start.7
  65.2 1.5 collective-permute-start.8
  66.7 7.0 %all-to-all-done = bf16[4,64,2048]{2,1,0:T(8,128)(2,1)} async-done(((bf16[4,64,2048]{2,1,0:T(8,128)(2,1)}), bf16[4,64,2048]{2,1,0:T(8,128)(2,1)}, u32[]{:S(2)}, u32[]{:S(2)}) %all-to-all-start) | async-done | bytes 1048608 | tf_op jit(solution)/shard_map/all_to_all | solution.py:405
  73.6 4.7 all-to-all-start.1
  78.4 1.2 select_select_fusion.1
  79.5 1.3 collective-permute-start.10
  80.8 0.7 collective-permute-start.11
  81.5 1.0 slice_convert_fusion
  82.5 0.7 collective-permute-start.21
  83.2 1.3 collective-permute-start.22
  85.1 58.0 %collective-permute-done.22 = s16[512,128]{1,0:T(8,128)(2,1)S(1)} collective-permute-done((s16[512,128]{1,0:T(8,128)(2,1)S(1)}, s16[512,128]{1,0:T(8,128)(2,1)S(1)}, u32[]{:S(2)}, u32[]{:S(2)}) %collective-permute-start.22) | collective-permute-done | bytes 131104 | tf_op jit(solution)/shard_map/ppermute | solution.py:356
  143.2 0.7 collective-permute-start.9
  143.8 0.0 collective-permute-done.10
  143.9 0.0 all-to-all-done.1
  143.9 1.9 collective-permute-start
  145.8 0.0 collective-permute-done.11
  145.8 3.9 collective-permute-start.3
  149.7 4.0 collective-permute-start.17
  153.8 1.8 collective-permute-start.20
  155.6 8.1 %fusion.7 = (f32[2560,128]{1,0:T(8,128)}, f32[2560,128]{1,0:T(8,128)}) fusion(s32[2560,128]{1,0:T(8,128)} %param.6, s32[]{:T(128)} %bitcast.8), kind=kLoop, calls=%fused_computation.18 | loop fusion | flops 4587520 | bytes 3932164 | tf_op jit(solution)/shard_map/cos | solution.py:351
  163.7 0.8 collective-permute-start.23
  164.5 0.9 select_select_fusion.refs_0_
  165.5 6.7 %collective-permute-done.refs_1_ = bf16[256,2048]{1,0:T(8,128)(2,1)} collective-permute-done((bf16[256,2048]{1,0:T(8,128)(2,1)}, bf16[256,2048]{1,0:T(8,128)(2,1)}, u32[]{:S(2)}, u32[]{:S(2)}) %collective-permute-start) | collective-permute-done | bytes 1048608 | tf_op jit(solution)/shard_map/ppermute | solution.py:356
  172.2 0.2 pad_maximum_fusion.steer_ref
  172.4 0.7 slice.30
  173.1 0.8 dynamic_slice.3
  173.9 0.6 reshape.22.refs_6_.refs_12_
  174.5 0.6 pad_add_fusion.spot_ref
  175.1 2.1 fusion.9
  177.1 0.9 pad_maximum_fusion.1.top_ref
  178.0 22.3 %collective-permute-done.17.refs_2_ = bf16[384,2048]{1,0:T(8,128)(2,1)} collective-permute-done((bf16[384,2048]{1,0:T(8,128)(2,1)}, bf16[384,2048]{1,0:T(8,128)(2,1)}, u32[]{:S(2)}, u32[]{:S(2)}) %collective-permute-start.17) | collective-permute-done | bytes 1572896 | tf_op jit(solution)/shard_map/ppermute | solution.py:356
  200.3 4.4 collective-permute-start.1
  204.7 3.4 collective-permute-start.4
  208.1 191.7 %shard_map.69 = bf16[1536,2048]{1,0:T(8,128)(2,1)} custom-call(s32[1]{0:T(128)} %bitcast.spot_ref, bf16[384,2048]{1,0:T(8,128)(2,1)} %slice.31.own, bf16[384,2048]{1,0:T(8,128)(2,1)} %collective-permute-done.15.refs_0_, bf16[384,2048]{1,0:T(8,128)(2,1)} %collective-permute-done.16.refs_1_, bf16[384,2048]{1,0:T(8,128)(2,1)} %collective-permute-done.17.refs_2_, ...), custom_call_target="tpu_custom_call" | custom-call | bytes 12582912 | tf_op jit(solution)/shard_map/pallas_call | solution.py:339
  399.8 5.2 all-to-all-start.2
  405.1 41.0 %shard_map.67 = (f32[512,512]{1,0:T(8,128)S(1)}, bf16[512,2048]{1,0:T(8,128)(2,1)S(1)}) custom-call(s32[1]{0:T(128)} %bitcast.1.spot_ref, bf16[128,2048]{1,0:T(8,128)(2,1)} %select_select_fusion.refs_0_, bf16[128,2048]{1,0:T(8,128)(2,1)} %collective-permute-done.12.refs_1_, bf16[128,2048]{1,0:T(8,128)(2,1)} %collective-permute-done.13.refs_2_, ...), custom_call_target="tpu_custom_call" | custom-call | flops 40000000000 | bytes 4000000 | tf_op jit(solution)/shard_map/pallas_call | solution.py:110
  446.1 1.0 copy-done.4
  447.1 1.3 copy-done.7
  448.4 2.3 collective-permute-start.2
  450.7 1.6 collective-permute-start.5
  452.3 1.2 copy-done.5
  453.6 1.6 copy-done.8
  455.1 19.7 %shard_map.68 = (f32[2560,512]{1,0:T(8,128)}, bf16[2560,512]{1,0:T(8,128)(2,1)S(1)}, bf16[2560,512]{1,0:T(8,128)(2,1)S(1)}) custom-call(s32[1]{0:T(128)S(6)} %mul.30.spot_ref, bf16[2560,2048]{1,0:T(8,128)(2,1)} %all-gather.2.cloned.1.call-done.rows_ref.refs_1_.refs_7_, bf16[512,2048]{1,0:T(8,128)(2,1)S(1)} %copy-done.8, f32[512,512]{1,0:T(8,128)S(1)} %copy-done.5, ...), custom_call_target="tpu_custom_call" | custom-call | flops 13421772800 | bytes 20971520 | tf_op jit(solution)/shard_map/pallas_call | solution.py:135
  474.9 1.5 copy-done
  476.4 1.5 copy-done.2
  477.9 48.1 %shard_map.70.refs_13_ = f32[2560,2560]{1,0:T(8,128)} custom-call(s32[2]{0:T(128)} %pad_add_fusion.spot_ref, bf16[1536,2048]{1,0:T(8,128)(2,1)} %bitcast.6.refs_0_, bf16[2560,2048]{1,0:T(8,128)(2,1)} %all-gather.2.cloned.1.call-done.rows_ref.refs_1_.refs_7_, bf16[2560,512]{1,0:T(8,128)(2,1)} %copy-done, bf16[2560,512]{1,0:T(8,128)(2,1)} %copy-done.2, ...), custom_call_target="tpu_custom_call" | custom-call | flops 28185722880 | bytes 26214400 | tf_op jit(solution)/shard_map/pallas_call | solution.py:249
  526.0 1.2 copy-done.6
  527.3 1.0 copy-done.9
  528.3 6.9 %shard_map.72 = f32[2,2560,128]{2,1,0:T(8,128)} custom-call(s32[1]{0:T(128)} %bitcast.spot_ref, f32[2560,256]{1,0:T(8,128)S(1)} %pad_maximum_fusion.steer_ref, f32[512,256]{1,0:T(8,128)S(1)} %copy-done.9, bf16[2560,512]{1,0:T(8,128)(2,1)S(1)} %copy-done.1, bf16[2560,512]{1,0:T(8,128)(2,1)S(1)} %copy-done.3, f32[512,512]{1,0:T(8,128)S(1)} %copy-done.6), custom_call_target="tpu_custom_call" | custom-call | flops 2013265920 | bytes 10485760 | tf_op jit(solution)/shard_map/pallas_call | solution.py:296
  535.2 33.1 %shard_map.71 = f32[2560,2560]{1,0:T(8,128)} custom-call(s32[2]{0:T(128)} %pad_add_fusion.spot_ref, bf16[256,2048]{1,0:T(8,128)(2,1)} %bitcast.3.refs_0_, bf16[256,2048]{1,0:T(8,128)(2,1)} %collective-permute-done.refs_1_, bf16[256,2048]{1,0:T(8,128)(2,1)} %collective-permute-done.1.refs_2_, ...), custom_call_target="tpu_custom_call", output_to_operand_aliasing={{}: (14, {})} | custom-call | flops 18790481920 | bytes 20971520 | tf_op jit(solution)/shard_map/pallas_call | solution.py:249
  (39 shorter events, 0.1 us)
Async XLA Ops:
  7.2 1.7 copy-start.10
  7.2 445.2 %all-gather.2.cloned.1.call-start = ((), (), s32[]{:S(2)}) async-start(), calls=%async_computation.3 | async-start | bytes 13107200 | tf_op jit(solution)/shard_map/all_gather | solution.py:399
  10.1 39.5 %collective-permute-start.15 = (bf16[384,2048]{1,0:T(8,128)(2,1)}, bf16[384,2048]{1,0:T(8,128)(2,1)}, u32[]{:S(2)}, u32[]{:S(2)}) collective-permute-start(bf16[384,2048]{1,0:T(8,128)(2,1)} %slice.31.own), channel_id=1, source_target_pairs={{0,8},{2,10},{4,12},{6,14},{8,16},{10,18},{12,20},{14,22},{16,24},... | collective-permute-start | bytes 4718600 | tf_op jit(solution)/shard_map/ppermute | solution.py:356
  13.6 39.5 %collective-permute-start.18 = (bf16[384,2048]{1,0:T(8,128)(2,1)}, bf16[384,2048]{1,0:T(8,128)(2,1)}, u32[]{:S(2)}, u32[]{:S(2)}) collective-permute-start(bf16[384,2048]{1,0:T(8,128)(2,1)} %slice.31.own), channel_id=1, source_target_pairs={{8,0},{10,2},{12,4},{14,6},{16,8},{18,10},{20,12},{22,14},{24,16},... | collective-permute-start | bytes 4718600 | tf_op jit(solution)/shard_map/ppermute | solution.py:356
  17.0 56.6 %all-to-all-start = ((bf16[4,64,2048]{2,1,0:T(8,128)(2,1)}), bf16[4,64,2048]{2,1,0:T(8,128)(2,1)}, u32[]{:S(2)}, u32[]{:S(2)}) async-start(bf16[4,64,2048]{2,1,0:T(8,128)(2,1)} %bitcast.13), calls=%async_computation | async-start | bytes 2097152 | tf_op jit(solution)/shard_map/all_to_all | solution.py:405
  49.6 100.1 %collective-permute-start.16 = (bf16[384,2048]{1,0:T(8,128)(2,1)}, bf16[384,2048]{1,0:T(8,128)(2,1)}, u32[]{:S(2)}, u32[]{:S(2)}) collective-permute-start(bf16[384,2048]{1,0:T(8,128)(2,1)} %collective-permute-done.15.refs_0_), channel_id=1, source_target_pairs={{8,16},{10,18},{12,20},{14,22},{16,24},{18,26},{20,28},{22,30},{9,... | collective-permute-start | bytes 4718600 | tf_op jit(solution)/shard_map/ppermute | solution.py:356
  53.2 100.6 %collective-permute-start.19 = (bf16[384,2048]{1,0:T(8,128)(2,1)}, bf16[384,2048]{1,0:T(8,128)(2,1)}, u32[]{:S(2)}, u32[]{:S(2)}) collective-permute-start(bf16[384,2048]{1,0:T(8,128)(2,1)} %collective-permute-done.18.refs_3_), channel_id=1, source_target_pairs={{8,0},{10,2},{12,4},{14,6},{16,8},{18,10},{20,12},{22,14},{9,1},{1... | collective-permute-start | bytes 4718600 | tf_op jit(solution)/shard_map/ppermute | solution.py:356
  62.3 16.1 %collective-permute-start.6 = (bf16[128,2048]{1,0:T(8,128)(2,1)}, bf16[128,2048]{1,0:T(8,128)(2,1)}, u32[]{:S(2)}, u32[]{:S(2)}) collective-permute-start(bf16[128,2048]{1,0:T(8,128)(2,1)} %get-tuple-element.15), channel_id=1, source_target_pairs={{0,2},{1,3}} | collective-permute-start | bytes 1572872 | tf_op jit(solution)/shard_map/ppermute | solution.py:356
  63.8 14.6 %collective-permute-start.7 = (bf16[128,2048]{1,0:T(8,128)(2,1)}, bf16[128,2048]{1,0:T(8,128)(2,1)}, u32[]{:S(2)}, u32[]{:S(2)}) collective-permute-start(bf16[128,2048]{1,0:T(8,128)(2,1)} %get-tuple-element.14), channel_id=1, source_target_pairs={{0,4},{1,5}} | collective-permute-start | bytes 1572872 | tf_op jit(solution)/shard_map/ppermute | solution.py:356
  65.2 13.1 %collective-permute-start.8 = (bf16[128,2048]{1,0:T(8,128)(2,1)S(1)}, bf16[128,2048]{1,0:T(8,128)(2,1)}, u32[]{:S(2)}, u32[]{:S(2)}) collective-permute-start(bf16[128,2048]{1,0:T(8,128)(2,1)S(1)} %get-tuple-element.13), channel_id=1, source_target_pairs={{0,6},{1,7}} | collective-permute-start | bytes 1572872 | tf_op jit(solution)/shard_map/ppermute | solution.py:356
  73.6 70.2 %all-to-all-start.1 = ((bf16[4,64,2048]{2,1,0:T(8,128)(2,1)}), bf16[4,64,2048]{2,1,0:T(8,128)(2,1)}, u32[]{:S(2)}, u32[]{:S(2)}) async-start(bf16[4,64,2048]{2,1,0:T(8,128)(2,1)} %all-to-all-done), calls=%async_computation.1 | async-start | bytes 2097152 | tf_op jit(solution)/shard_map/all_to_all | solution.py:406
  79.5 64.3 %collective-permute-start.10 = (bf16[128,2048]{1,0:T(8,128)(2,1)S(1)}, bf16[128,2048]{1,0:T(8,128)(2,1)S(1)}, u32[]{:S(2)}, u32[]{:S(2)}) collective-permute-start(bf16[128,2048]{1,0:T(8,128)(2,1)S(1)} %select_select_fusion.1), channel_id=1, source_target_pairs={{0,16},{2,18},{4,20},{6,22},{1,17},{3,19},{5,21},{7,23}} | collective-permute-start | bytes 1572872 | tf_op jit(solution)/shard_map/ppermute | solution.py:356
  80.8 65.0 %collective-permute-start.11 = (bf16[128,2048]{1,0:T(8,128)(2,1)S(1)}, bf16[128,2048]{1,0:T(8,128)(2,1)S(1)}, u32[]{:S(2)}, u32[]{:S(2)}) collective-permute-start(bf16[128,2048]{1,0:T(8,128)(2,1)S(1)} %select_select_fusion.1), channel_id=1, source_target_pairs={{0,24},{2,26},{4,28},{6,30},{1,25},{3,27},{5,29},{7,31}} | collective-permute-start | bytes 1572872 | tf_op jit(solution)/shard_map/ppermute | solution.py:356
  82.5 0.7 collective-permute-start.21
  83.2 60.0 %collective-permute-start.22 = (s16[512,128]{1,0:T(8,128)(2,1)S(1)}, s16[512,128]{1,0:T(8,128)(2,1)S(1)}, u32[]{:S(2)}, u32[]{:S(2)}) collective-permute-start(s16[512,128]{1,0:T(8,128)(2,1)S(1)} %slice_convert_fusion), channel_id=1, source_target_pairs={{0,16},{2,18},{4,20},{6,22},{1,17},{3,19},{5,21},{7,23}} | collective-permute-start | bytes 393224 | tf_op jit(solution)/shard_map/ppermute | solution.py:356
  143.2 20.6 %collective-permute-start.9 = (bf16[128,2048]{1,0:T(8,128)(2,1)S(1)}, bf16[128,2048]{1,0:T(8,128)(2,1)S(1)}, u32[]{:S(2)}, u32[]{:S(2)}) collective-permute-start(bf16[128,2048]{1,0:T(8,128)(2,1)S(1)} %select_select_fusion.1), channel_id=1, source_target_pairs={{0,8},{2,10},{4,12},{6,14},{1,9},{3,11},{5,13},{7,15}} | collective-permute-start | bytes 1572872 | tf_op jit(solution)/shard_map/ppermute | solution.py:356
  143.9 28.3 %collective-permute-start = (bf16[256,2048]{1,0:T(8,128)(2,1)}, bf16[256,2048]{1,0:T(8,128)(2,1)}, u32[]{:S(2)}, u32[]{:S(2)}) collective-permute-start(bf16[256,2048]{1,0:T(8,128)(2,1)} %bitcast.3.refs_0_), channel_id=1, source_target_pairs={{0,8},{2,10},{4,12},{6,14},{8,16},{10,18},{12,20},{14,22},{16,24},... | collective-permute-start | bytes 3145736 | tf_op jit(solution)/shard_map/ppermute | solution.py:356
  145.8 26.4 %collective-permute-start.3 = (bf16[256,2048]{1,0:T(8,128)(2,1)}, bf16[256,2048]{1,0:T(8,128)(2,1)}, u32[]{:S(2)}, u32[]{:S(2)}) collective-permute-start(bf16[256,2048]{1,0:T(8,128)(2,1)} %bitcast.3.refs_0_), channel_id=1, source_target_pairs={{8,0},{10,2},{12,4},{14,6},{16,8},{18,10},{20,12},{22,14},{24,16},... | collective-permute-start | bytes 3145736 | tf_op jit(solution)/shard_map/ppermute | solution.py:356
  149.7 50.5 %collective-permute-start.17 = (bf16[384,2048]{1,0:T(8,128)(2,1)}, bf16[384,2048]{1,0:T(8,128)(2,1)}, u32[]{:S(2)}, u32[]{:S(2)}) collective-permute-start(bf16[384,2048]{1,0:T(8,128)(2,1)} %collective-permute-done.16.refs_1_), channel_id=1, source_target_pairs={{16,24},{18,26},{20,28},{22,30},{17,25},{19,27},{21,29},{23,31}} | collective-permute-start | bytes 4718600 | tf_op jit(solution)/shard_map/ppermute | solution.py:356
  153.8 50.9 %collective-permute-start.20 = (bf16[384,2048]{1,0:T(8,128)(2,1)}, bf16[384,2048]{1,0:T(8,128)(2,1)}, u32[]{:S(2)}, u32[]{:S(2)}) collective-permute-start(bf16[384,2048]{1,0:T(8,128)(2,1)} %collective-permute-done.19.refs_4_), channel_id=1, source_target_pairs={{8,0},{10,2},{12,4},{14,6},{9,1},{11,3},{13,5},{15,7}} | collective-permute-start | bytes 4718600 | tf_op jit(solution)/shard_map/ppermute | solution.py:356
  163.7 8.5 %copy-start.11 = (f32[2560,128]{1,0:T(8,128)S(1)}, f32[2560,128]{1,0:T(8,128)}, u32[]{:S(2)}) copy-start(f32[2560,128]{1,0:T(8,128)} %get-tuple-element.16) | copy-start | bytes 3932164
  163.7 8.5 %copy-start.12 = (f32[2560,128]{1,0:T(8,128)S(1)}, f32[2560,128]{1,0:T(8,128)}, u32[]{:S(2)}) copy-start(f32[2560,128]{1,0:T(8,128)} %get-tuple-element.17) | copy-start | bytes 3932164
  163.7 1.7 collective-permute-start.23
  165.5 239.6 %collective-permute-start.12 = (bf16[128,2048]{1,0:T(8,128)(2,1)}, bf16[128,2048]{1,0:T(8,128)(2,1)}, u32[]{:S(2)}, u32[]{:S(2)}) collective-permute-start(bf16[128,2048]{1,0:T(8,128)(2,1)} %select_select_fusion.refs_0_), channel_id=1, source_target_pairs={{0,2},{2,0},{4,6},{6,4},{8,10},{10,8},{12,14},{14,12},{16,18},{18,... | collective-permute-start | bytes 1572872 | tf_op jit(solution)/shard_map/ppermute | solution.py:356
  172.2 232.9 %collective-permute-start.13 = (bf16[128,2048]{1,0:T(8,128)(2,1)}, bf16[128,2048]{1,0:T(8,128)(2,1)}, u32[]{:S(2)}, u32[]{:S(2)}) collective-permute-start(bf16[128,2048]{1,0:T(8,128)(2,1)} %select_select_fusion.refs_0_), channel_id=1, source_target_pairs={{0,4},{2,6},{4,0},{6,2},{8,12},{10,14},{12,8},{14,10},{16,20},{18,... | collective-permute-start | bytes 1572872 | tf_op jit(solution)/shard_map/ppermute | solution.py:356
  172.2 232.9 %collective-permute-start.14 = (bf16[128,2048]{1,0:T(8,128)(2,1)}, bf16[128,2048]{1,0:T(8,128)(2,1)}, u32[]{:S(2)}, u32[]{:S(2)}) collective-permute-start(bf16[128,2048]{1,0:T(8,128)(2,1)} %select_select_fusion.refs_0_), channel_id=1, source_target_pairs={{0,6},{2,4},{4,2},{6,0},{8,14},{10,12},{12,10},{14,8},{16,22},{18,... | collective-permute-start | bytes 1572872 | tf_op jit(solution)/shard_map/ppermute | solution.py:356
  200.3 248.1 %collective-permute-start.1 = (bf16[256,2048]{1,0:T(8,128)(2,1)}, bf16[256,2048]{1,0:T(8,128)(2,1)}, u32[]{:S(2)}, u32[]{:S(2)}) collective-permute-start(bf16[256,2048]{1,0:T(8,128)(2,1)} %collective-permute-done.refs_1_), channel_id=1, source_target_pairs={{8,16},{10,18},{12,20},{14,22},{16,24},{18,26},{20,28},{22,30},{9,... | collective-permute-start | bytes 3145736 | tf_op jit(solution)/shard_map/ppermute | solution.py:356
  204.7 246.0 %collective-permute-start.4 = (bf16[256,2048]{1,0:T(8,128)(2,1)}, bf16[256,2048]{1,0:T(8,128)(2,1)}, u32[]{:S(2)}, u32[]{:S(2)}) collective-permute-start(bf16[256,2048]{1,0:T(8,128)(2,1)} %collective-permute-done.3.refs_4_), channel_id=1, source_target_pairs={{8,0},{10,2},{12,4},{14,6},{16,8},{18,10},{20,12},{22,14},{9,1},{1... | collective-permute-start | bytes 3145736 | tf_op jit(solution)/shard_map/ppermute | solution.py:356
  399.8 78.1 %all-to-all-start.2 = ((bf16[4,384,2048]{2,1,0:T(8,128)(2,1)}), bf16[4,384,2048]{2,1,0:T(8,128)(2,1)}, u32[]{:S(2)}, u32[]{:S(2)}) async-start(bf16[4,384,2048]{2,1,0:T(8,128)(2,1)} %bitcast.12), calls=%async_computation.2 | async-start | bytes 12582912 | tf_op jit(solution)/shard_map/all_to_all | solution.py:404
  446.1 1.0 copy-start.4
  447.1 1.3 copy-start.7
  448.4 86.7 %collective-permute-start.2 = (bf16[256,2048]{1,0:T(8,128)(2,1)}, bf16[256,2048]{1,0:T(8,128)(2,1)}, u32[]{:S(2)}, u32[]{:S(2)}) collective-permute-start(bf16[256,2048]{1,0:T(8,128)(2,1)} %collective-permute-done.1.refs_2_), channel_id=1, source_target_pairs={{16,24},{18,26},{20,28},{22,30},{17,25},{19,27},{21,29},{23,31}} | collective-permute-start | bytes 3145736 | tf_op jit(solution)/shard_map/ppermute | solution.py:356
  450.7 84.5 %collective-permute-start.5 = (bf16[256,2048]{1,0:T(8,128)(2,1)}, bf16[256,2048]{1,0:T(8,128)(2,1)}, u32[]{:S(2)}, u32[]{:S(2)}) collective-permute-start(bf16[256,2048]{1,0:T(8,128)(2,1)} %collective-permute-done.4.refs_5_), channel_id=1, source_target_pairs={{8,0},{10,2},{12,4},{14,6},{9,1},{11,3},{13,5},{15,7}} | collective-permute-start | bytes 3145736 | tf_op jit(solution)/shard_map/ppermute | solution.py:356
  452.3 1.2 copy-start.5
  453.6 1.6 copy-start.8
  474.9 1.5 copy-start
  476.4 1.5 copy-start.2
  477.9 48.1 %copy-start.1 = (bf16[2560,512]{1,0:T(8,128)(2,1)S(1)}, bf16[2560,512]{1,0:T(8,128)(2,1)}, u32[]{:S(2)}) copy-start(bf16[2560,512]{1,0:T(8,128)(2,1)} %copy-done) | copy-start | bytes 7864324
  477.9 48.1 %copy-start.3 = (bf16[2560,512]{1,0:T(8,128)(2,1)S(1)}, bf16[2560,512]{1,0:T(8,128)(2,1)}, u32[]{:S(2)}) copy-start(bf16[2560,512]{1,0:T(8,128)(2,1)} %copy-done.2) | copy-start | bytes 7864324
  526.0 1.2 copy-start.6
  527.3 1.0 copy-start.9
Sparse Core Ops, SparseCore 0:
  9.8 116.3 all-gather.1

commit v2 on v1

--- a/solution.py
+++ b/solution.py
@@ -118,42 +118,69 @@
     )(spot, *pieces, load)
 
 
-def panel_kernel(snap, spot_ref, rows_ref, head_ref, inv_ref, load_ref, panel_ref, high_ref, low_ref):
+def panel_kernel(snap, spot_ref, rows_ref, head_ref, inv_ref, load_ref, steer_ref, top_ref, *refs):
+    panel_ref, high_ref, low_ref, white_ref, solved = refs
+    step = pl.program_id(0)
+    tile = rows_ref.shape[0]
+
+    @pl.when(step == 0)
+    def _():
+        solved[...] = jnp.dot(inv_ref[...], top_ref[...], precision=HIGHEST, preferred_element_type=F32)
+
     side = dot_nt(rows_ref[...], head_ref[...]) / snap
-    row = lax.broadcasted_iota(jnp.int32, side.shape, 0) + (spot_ref[0] + pl.program_id(0) * side.shape[0])
+    row = lax.broadcasted_iota(jnp.int32, side.shape, 0) + (spot_ref[0] * (tile * pl.num_programs(0)) + step * tile)
     side = side + jnp.where(row == lax.broadcasted_iota(jnp.int32, side.shape, 1), load_ref[...], 0.0)
     panel = dot_nt(side, inv_ref[...], HIGHEST)
     panel_ref[...] = panel
     high, low = split(panel)
     high_ref[...] = high
     low_ref[...] = low
-
-
-def own_panel(first, rows, head, inv, load, snap, tile):
+    s_high, s_low = split(solved[...])
+    below = steer_ref[...]
+    below -= jnp.dot(high, s_high, preferred_element_type=F32)
+    below -= jnp.dot(high, s_low, preferred_element_type=F32)
+    below -= jnp.dot(low, s_high, preferred_element_type=F32)
+    half = below.shape[1] // 2
+    white_ref[0] = below[:, :half]
+    white_ref[1] = below[:, half:]
+
+    @pl.when((spot_ref[0] == 0) & (step * tile < PANEL))
+    def _():
+        mine = solved[pl.ds(pl.multiple_of(step * tile, tile), tile), :]
+        white_ref[0] = mine[:, :half]
+        white_ref[1] = mine[:, half:]
+
+
+def own_panel(spot, rows, head, inv, load, steer, top, snap, tile):
     n, depth = rows.shape
     width = head.shape[0]
+    vectors = steer.shape[1]
     return pl.pallas_call(
         functools.partial(panel_kernel, snap),
         grid=(n // tile,),
-        out_shape=tuple(jax.ShapeDtypeStruct((n, width), t) for t in (F32, BF16, BF16)),
+        out_shape=tuple(jax.ShapeDtypeStruct((n, width), t) for t in (F32, BF16, BF16))
+        + (jax.ShapeDtypeStruct((2, n, vectors // 2), F32),),
         in_specs=[
             SMEM,
             vmem((tile, depth), lambda i: (i, 0)),
             vmem((width, depth), lambda i: (0, 0)),
             vmem((width, width), lambda i: (0, 0)),
             vmem((1, width), lambda i: (0, 0)),
+            vmem((tile, vectors), lambda i: (i, 0)),
+            vmem((width, vectors), lambda i: (0, 0)),
         ],
-        out_specs=tuple(vmem((tile, width), lambda i: (i, 0)) for _ in range(3)),
-        compiler_params=pltpu.CompilerParams(vmem_limit_bytes=40 << 20),
+        out_specs=tuple(vmem((tile, width), lambda i: (i, 0)) for _ in range(3))
+        + (vmem((2, tile, vectors // 2), lambda i: (0, i, 0)),),
+        scratch_shapes=[pltpu.VMEM((width, vectors), F32)],
+        compiler_params=pltpu.CompilerParams(vmem_limit_bytes=48 << 20),
         cost_estimate=cost(2 * n * width * (depth + 6 * width), 2 * n * depth + 8 * n * width),
-    )(first, rows, head, inv, load)
+    )(spot, rows, head, inv, load, steer, top)
 
 
 def trailing_kernel(snap, geo, gather, spot_ref, *refs):
     tile, groups, width, stride, first, size = geo
-    parts = 7 if gather else 1
-    sources = refs[:parts]
-    rows_ref, high_ref, low_ref, head_ref, inv_ref, load_ref = refs[parts : parts + 6]
+    source = refs[0]
+    rows_ref, high_ref, low_ref, head_ref, inv_ref, load_ref = refs[1:7]
     out_ref, cols_ref, col_high, col_low, acc, out_sem, in_sem = refs[len(refs) - 7 :]
     row_at, col_at = spot_ref[0], spot_ref[1]
     step, steps = pl.program_id(0), pl.num_programs(0)
@@ -172,36 +199,25 @@
 
     @pl.when(step == 0)
     def _():
-        if gather:
-            own, ups, downs = sources[0], sources[1:4], sources[4:7]
-            piece = width // 4
-
-            def pull(src, plane):
-                for g in range(groups):
+        piece = width // groups
+        for g in range(groups):
+            if gather:
+                for k in range(groups):
                     pltpu.make_async_copy(
-                        src.at[pl.ds(g * piece, piece)],
-                        cols_ref.at[pl.ds(pl.multiple_of(g * width + plane * piece, piece), piece)],
-                        in_sem,
+                        source.at[pl.ds((k * groups + g) * piece, piece)],
+                        cols_ref.at[pl.ds(g * width + k * piece, piece)],
+                        in_sem.at[g],
                     ).start()
-
-            pull(own, row_at)
-            for j in range(1, 4):
-
-                @pl.when(row_at >= j)
-                def _(j=j):
-                    pull(ups[j - 1], row_at - j)
-
-                @pl.when(row_at < j)
-                def _(j=j):
-                    pull(downs[3 - j], row_at - j + 4)
-
-        else:
-            pltpu.make_async_copy(sources[0], cols_ref, in_sem).start()
-        pltpu.make_async_copy(cols_ref, cols_ref, in_sem).wait()
-        side = dot_nt(cols_ref[...], head_ref[...]) / snap
-        high, low = split(dot_nt(side, inv_ref[...], HIGHEST))
-        col_high[...] = high
-        col_low[...] = low
+            else:
+                part = pl.ds(g * width, width)
+                pltpu.make_async_copy(source.at[part], cols_ref.at[part], in_sem.at[g]).start()
+        for g in range(groups):
+            part = pl.ds(g * width, width)
+            pltpu.make_async_copy(cols_ref.at[part], cols_ref.at[part], in_sem.at[g]).wait()
+            side = dot_nt(cols_ref[part, :], head_ref[...]) / snap
+            high, low = split(dot_nt(side, inv_ref[...], HIGHEST))
+            col_high[part, :] = high
+            col_low[part, :] = low
 
     @pl.when(step >= 2)
     def _():
@@ -226,14 +242,13 @@
             pltpu.make_async_copy(acc.at[k], acc.at[k], out_sem.at[k]).wait()
 
 
-def trailing_part(spot, sources, rows, high, low, head, inv, load, so_far, snap, geo):
+def trailing_part(spot, source, gather, rows, high, low, head, inv, load, so_far, snap, geo):
     tile, groups, width, stride, first, size = geo
     n, depth = rows.shape
     panel = head.shape[0]
     count = groups * width
-    gather = len(sources) > 1
-    given = [spot, *sources, rows, high, low, head, inv, load]
-    specs = [SMEM] + [ANY] * len(sources) + [
+    given = [spot, source, rows, high, low, head, inv, load]
+    specs = [SMEM, ANY,
         vmem((tile, depth), lambda i: (i, 0)),
         vmem((tile, panel), lambda i: (i, 0)),
         vmem((tile, panel), lambda i: (i, 0)),
@@ -258,7 +273,7 @@
             pltpu.VMEM((count, panel), BF16),
             pltpu.VMEM((2, tile, count), F32),
             pltpu.SemaphoreType.DMA((2,)),
-            pltpu.SemaphoreType.DMA,
+            pltpu.SemaphoreType.DMA((groups,)),
         ],
         input_output_aliases=alias,
         compiler_params=pltpu.CompilerParams(vmem_limit_bytes=56 << 20),
@@ -266,72 +281,34 @@
     )(*given)
 
 
-def steer_kernel(spot_ref, steer_ref, top_ref, high_ref, low_ref, inv_ref, out_ref, solved):
-    step = pl.program_id(0)
-    tile = steer_ref.shape[0]
-
-    @pl.when(step == 0)
-    def _():
-        solved[...] = jnp.dot(inv_ref[...], top_ref[...], precision=HIGHEST, preferred_element_type=F32)
-
-    s_high, s_low = split(solved[...])
-    below = steer_ref[...]
-    below -= jnp.dot(high_ref[...], s_high, preferred_element_type=F32)
-    below -= jnp.dot(high_ref[...], s_low, preferred_element_type=F32)
-    below -= jnp.dot(low_ref[...], s_high, preferred_element_type=F32)
-    half = below.shape[1] // 2
-    out_ref[0] = below[:, :half]
-    out_ref[1] = below[:, half:]
-
-    @pl.when((spot_ref[0] == 0) & (step * tile < PANEL))
-    def _():
-        mine = solved[pl.ds(pl.multiple_of(step * tile, tile), tile), :]
-        out_ref[0] = mine[:, :half]
-        out_ref[1] = mine[:, half:]
-
-
-def whiten(spot, steer, top, high, low, inv, tile):
-    n, width = steer.shape
-    panel = inv.shape[0]
-    return pl.pallas_call(
-        steer_kernel,
-        grid=(n // tile,),
-        out_shape=jax.ShapeDtypeStruct((2, n, width // 2), F32),
-        in_specs=[
-            SMEM,
-            vmem((tile, width), lambda i: (i, 0)),
-            vmem((panel, width), lambda i: (0, 0)),
-            vmem((tile, panel), lambda i: (i, 0)),
-            vmem((tile, panel), lambda i: (i, 0)),
-            vmem((panel, panel), lambda i: (0, 0)),
-        ],
-        out_specs=vmem((2, tile, width // 2), lambda i: (0, i, 0)),
-        scratch_shapes=[pltpu.VMEM((panel, width), F32)],
-        compiler_params=pltpu.CompilerParams(vmem_limit_bytes=40 << 20),
-        cost_estimate=cost(6 * n * panel * width, 8 * n * width + 4 * n * panel),
-    )(spot, steer, top, high, low, inv)
-
-
 def line_kernel(spot_ref, own, *refs):
-    ups, downs, out, sem = refs[:3], refs[3:6], refs[6], refs[7]
+    ups, downs, out, held, in_sem, out_sem = refs[:3], refs[3:6], refs[6], refs[7], refs[8], refs[9]
     n = own.shape[0]
     at = spot_ref[0]
 
-    def put(src, plane):
-        pltpu.make_async_copy(src, out.at[pl.ds(pl.multiple_of(plane * n, n), n)], sem).start()
-
-    put(own, at)
+    def pull(src, k):
+        pltpu.make_async_copy(src, held.at[k], in_sem.at[k]).start()
+
+    pull(own, 0)
     for j in range(1, 4):
 
         @pl.when(at >= j)
         def _(j=j):
-            put(ups[j - 1], at - j)
+            pull(ups[j - 1], j)
 
         @pl.when(at < j)
         def _(j=j):
-            put(downs[3 - j], at - j + 4)
-
-    pltpu.make_async_copy(out, out, sem).wait()
+            pull(downs[3 - j], j)
+
+    pushes = []
+    for j in range(4):
+        pltpu.make_async_copy(held.at[j], held.at[j], in_sem.at[j]).wait()
+        plane = jnp.where(at >= j, at - j, at - j + 4)
+        push = pltpu.make_async_copy(held.at[j], out.at[pl.ds(pl.multiple_of(plane * n, n), n)], out_sem.at[j])
+        push.start()
+        pushes.append(push)
+    for push in pushes:
+        push.wait()
 
 
 def in_line(spot, own, ups, downs):
@@ -341,9 +318,18 @@
         out_shape=jax.ShapeDtypeStruct((4 * n, depth), own.dtype),
         in_specs=[SMEM] + [ANY] * 7,
         out_specs=ANY,
-        scratch_shapes=[pltpu.SemaphoreType.DMA],
+        scratch_shapes=[
+            pltpu.VMEM((4, n, depth), own.dtype),
+            pltpu.SemaphoreType.DMA((4,)),
+            pltpu.SemaphoreType.DMA((4,)),
+        ],
+        compiler_params=pltpu.CompilerParams(vmem_limit_bytes=24 << 20),
         cost_estimate=cost(0, 16 * n * depth),
     )(spot, own, *ups, *downs)
+
+
+def after(value, *others):
+    return lax.optimization_barrier((value, *others))[0]
 
 
 def steer_of(delays, bin_index):
@@ -362,12 +348,8 @@
         planes = [r for r in range(count) if 0 <= r + way < count and 0 <= r - way * (k - 1) < count]
         return [((r, p), (r + way, p)) for r in planes for p in range(count)]
 
-    def line(own):
-        ups, downs = [own], [own]
-        for k in range(1, count):
-            ups.append(move(ups[-1], along(k, 1)))
-            downs.append(move(downs[-1], along(k, -1)))
-        return ups[1:], downs[1:]
+    def hop(value, k):
+        return [move(value[0], along(k, 1)), move(value[1], along(k, -1))]
 
     def chosen(index, values):
         out = values[-1]
@@ -386,39 +368,45 @@
 
         quarter = PANEL // count
         quarters = [lax.slice_in_dim(spectra, j * quarter, (j + 1) * quarter) for j in range(count)]
+        first = spectra[:early]
+        head_load = loading[:PANEL].reshape(1, PANEL)
+
+        own_rows = lax.all_gather(spectra, "col", axis=0, tiled=True)
+        one = hop([first, first], 1)
         held = chosen(col, [quarters[0]] + [move(quarters[j], [((0, 0), (0, j))]) for j in range(1, count)])
-        lifted = [held] + [move(held, [((0, p), (k, p)) for p in range(count)]) for k in range(1, count)]
-        piece = chosen(row, lifted)
-        pieces = [piece] + [move(piece, across(m)) for m in range(1, count)]
-
         top = delays[:PANEL].astype(jnp.int16)
         tops = [top] + [move(top, [((0, p), (k, p)) for p in range(count)]) for k in range(1, count)]
+
+        held = after(held, *one, *tops)
+        lifted = [held] + [move(held, [((0, p), (k, p)) for p in range(count)]) for k in range(1, count)]
+        two = hop([after(v, held) for v in one], 2)
+        rest = lax.all_to_all(after(spectra[early:], held), "row", 0, 0, tiled=True)
+        piece = after(chosen(row, lifted), *two)
+
+        pieces = [piece] + [move(piece, across(m)) for m in range(1, count)]
+        three = hop([after(v, piece) for v in two], 3)
+        rest = lax.all_to_all(after(rest, piece), "col", 0, 0, tiled=True)
+        three = [after(v, *pieces) for v in three]
+        stacked = in_line(spot_row, first, [one[0], two[0], three[0]], [one[1], two[1], three[1]])
+        cols_first = lax.all_to_all(stacked, "col", 0, 0, tiled=True)
+        cols_rest = lax.all_gather(after(rest, stacked), "row", axis=0, tiled=True)
+
+        pieces = [after(v, stacked) for v in pieces]
+        inv, head = head_factor(col.astype(jnp.int32).reshape(1), pieces, head_load, snap)
         steer_top = steer_of(chosen(row, tops).astype(jnp.int32), bin_index[0])
         steer = steer_of(delays, bin_index[0])
-
-        own_rows = lax.all_gather(spectra, "col", axis=0, tiled=True)
-
-        first = spectra[:early]
-        ups, downs = line(first)
-        stacked = in_line(spot_row, first, ups, downs)
-        cols_first = lax.all_to_all(stacked, "col", 0, 0, tiled=True)
-        rest = lax.all_to_all(spectra[early:], "row", 0, 0, tiled=True)
-        rest = lax.all_to_all(rest, "col", 0, 0, tiled=True)
-        rest_ups, rest_downs = line(rest)
-
-        head_load = loading[:PANEL].reshape(1, PANEL)
-        inv, head = head_factor(col.astype(jnp.int32).reshape(1), pieces, head_load, snap)
-        panel, high, low = own_panel(spot_row * size, own_rows, head, inv, head_load, snap, size // 10)
-        whitened = whiten(spot_row, steer, steer_top, high, low, inv, PANEL // 2)
+        panel, high, low, whitened = own_panel(
+            spot_row, after(own_rows, rest), head, inv, head_load, steer, steer_top, snap, PANEL
+        )
 
         load = lax.dynamic_slice_in_dim(loading, col * size, size).reshape(1, size)
         tile = size // 8
         trailing = trailing_part(
-            spot, [cols_first], own_rows, high, low, head, inv, load, None, snap,
+            spot, cols_first, False, own_rows, high, low, head, inv, load, None, snap,
             (tile, count, early, block, 0, size),
         )
         trailing = trailing_part(
-            spot, [rest, *rest_ups, *rest_downs], own_rows, high, low, head, inv, load, trailing, snap,
+            spot, cols_rest, True, own_rows, high, low, head, inv, load, trailing, snap,
             (tile, count, block - early, block, early, size),
         )
         return (trailing, panel, whitened)

time: 576 us -> 347 us (0.60)
  the two profiles are of different devices: /device:TPU:22 before, /device:TPU:0 now
where the time goes in v2:
time: 347 us; the launch traced here: 340 us
  Pallas kernels  145 us (42%)
  waiting for transfers between devices  91.3 us (26%)
  starting transfers between devices  58.4 us (17%)
  other arithmetic  18.2 us (5%)
  between operations  15 us (4%)
  local copies, waits for them, and re-layouts  11.4 us (3%)
    ppermute x18, waiting for transfers between devices, move(): lax.ppermute(value, ('row', 'col'), [(a * count + b, c * count + d) for (...  88.1 us
    pallas_call x2, Pallas kernels, trailing_part(): pl.pallas_call(functools.partial(trailing_kernel, snap, geo, gather), gri...  79.9 us
    ppermute x18, starting transfers between devices, move(): lax.ppermute(value, ('row', 'col'), [(a * count + b, c * count + d) for (...  44.4 us
    pallas_call x1, Pallas kernels, head_factor(): pl.pallas_call(functools.partial(factor_kernel, snap, len(pieces)), out_s...  41 us
    pallas_call x1, Pallas kernels, own_panel(): pl.pallas_call(functools.partial(panel_kernel, snap), grid=(n // tile,),...  22.2 us
    cos x2, other arithmetic, steer_of(): return jnp.concatenate([jnp.cos(angle), jnp.sin(angle)], axis=1)  8.24 us
  transfers between devices with their start and end apart: 23, of which 11 were waited for; matrix products, arithmetic and copies ran while one was open for 8% of the time, Pallas kernels for 33%

profile of v2, /device:TPU:0, one launch (start us, length us, event | category | flops | bytes accessed | tf_op | source)
XLA Modules:
  0.0 339.8 jit_solution(9485709052853593947)
XLA Ops:
  7.2 0.0 all-gather.5.cloned.1.call-start
  7.2 0.7 all-gather.5.cloned.1.call-update
  7.9 0.0 copy-start.4
  7.9 1.7 slice.30.own
  9.6 1.3 collective-permute-start.4
  10.9 6.7 %collective-permute-start.3 = (bf16[384,2048]{1,0:T(8,128)(2,1)S(1)}, bf16[384,2048]{1,0:T(8,128)(2,1)}, u32[]{:S(2)}, u32[]{:S(2)}) collective-permute-start(bf16[384,2048]{1,0:T(8,128)(2,1)S(1)} %slice.30.own), channel_id=1, source_target_pairs={{0,8},{2,10},{4,12},{6,14},{8,16},{10,18},{12,20},{14,22},{16,24},... | collective-permute-start | bytes 4718600 | tf_op jit(solution)/shard_map/ppermute | solution.py:342
  17.7 1.2 fusion.10
  18.8 5.6 %collective-permute-start.2 = (bf16[128,2048]{1,0:T(8,128)(2,1)}, bf16[128,2048]{1,0:T(8,128)(2,1)}, u32[]{:S(2)}, u32[]{:S(2)}) collective-permute-start(bf16[128,2048]{1,0:T(8,128)(2,1)} %get-tuple-element.47), channel_id=1, source_target_pairs={{0,6},{1,7}} | collective-permute-start | bytes 1572872 | tf_op jit(solution)/shard_map/ppermute | solution.py:342
  24.4 2.1 collective-permute-start.1
  26.5 2.1 collective-permute-start
  28.6 1.0 slice_convert_fusion
  29.6 17.8 %collective-permute-done.2 = bf16[128,2048]{1,0:T(8,128)(2,1)} collective-permute-done((bf16[128,2048]{1,0:T(8,128)(2,1)}, bf16[128,2048]{1,0:T(8,128)(2,1)}, u32[]{:S(2)}, u32[]{:S(2)}) %collective-permute-start.2) | collective-permute-done | bytes 524320 | tf_op jit(solution)/shard_map/ppermute | solution.py:342
  47.4 1.3 collective-permute-start.7
  48.7 0.2 collective-permute-done.1
  49.0 1.3 collective-permute-start.6
  50.3 19.0 %collective-permute-done = bf16[128,2048]{1,0:T(8,128)(2,1)} collective-permute-done((bf16[128,2048]{1,0:T(8,128)(2,1)}, bf16[128,2048]{1,0:T(8,128)(2,1)}, u32[]{:S(2)}, u32[]{:S(2)}) %collective-permute-start) | collective-permute-done | bytes 524320 | tf_op jit(solution)/shard_map/ppermute | solution.py:342
  69.2 1.3 collective-permute-start.5
  70.5 2.1 select_select_fusion.1
  72.6 0.0 collective-permute-done.7
  72.6 0.0 collective-permute-done.6
  72.6 0.4 collective-permute-done.5
  73.0 1.8 collective-permute-start.11
  74.9 1.3 collective-permute-start.12
  76.1 2.1 collective-permute-start.10
  78.3 8.4 %collective-permute-start.9 = (bf16[128,2048]{1,0:T(8,128)(2,1)}, bf16[128,2048]{1,0:T(8,128)(2,1)}, u32[]{:S(2)}, u32[]{:S(2)}) collective-permute-start(bf16[128,2048]{1,0:T(8,128)(2,1)} %select_select_fusion.1), channel_id=1, source_target_pairs={{0,16},{2,18},{4,20},{6,22},{1,17},{3,19},{5,21},{7,23}} | collective-permute-start | bytes 1572872 | tf_op jit(solution)/shard_map/ppermute | solution.py:342
  86.6 2.1 collective-permute-start.8
  88.7 2.3 slice.25
  91.0 4.3 %all-to-all-start = ((bf16[4,64,2048]{2,1,0:T(8,128)(2,1)}), bf16[4,64,2048]{2,1,0:T(8,128)(2,1)}, u32[]{:S(2)}, u32[]{:S(2)}) async-start(bf16[4,64,2048]{2,1,0:T(8,128)(2,1)} %bitcast.15), calls=%async_computation | async-start | bytes 2097152 | tf_op jit(solution)/shard_map/all_to_all | solution.py:383
  95.3 0.0 copy-start.5
  96.0 5.3 %collective-permute-done.9 = bf16[128,2048]{1,0:T(8,128)(2,1)} collective-permute-done((bf16[128,2048]{1,0:T(8,128)(2,1)}, bf16[128,2048]{1,0:T(8,128)(2,1)}, u32[]{:S(2)}, u32[]{:S(2)}) %collective-permute-start.9) | collective-permute-done | bytes 524320 | tf_op jit(solution)/shard_map/ppermute | solution.py:342
  101.4 11.2 %collective-permute-done.8 = bf16[128,2048]{1,0:T(8,128)(2,1)} collective-permute-done((bf16[128,2048]{1,0:T(8,128)(2,1)}, bf16[128,2048]{1,0:T(8,128)(2,1)}, u32[]{:S(2)}, u32[]{:S(2)}) %collective-permute-start.8) | collective-permute-done | bytes 524320 | tf_op jit(solution)/shard_map/ppermute | solution.py:342
  112.6 2.1 select_select_fusion.refs_0_
  114.7 5.4 %collective-permute-done.12.refs_4_ = bf16[384,2048]{1,0:T(8,128)(2,1)} collective-permute-done((bf16[384,2048]{1,0:T(8,128)(2,1)S(1)}, bf16[384,2048]{1,0:T(8,128)(2,1)}, u32[]{:S(2)}, u32[]{:S(2)}) %collective-permute-start.12) | collective-permute-done | bytes 1572896 | tf_op jit(solution)/shard_map/ppermute | solution.py:342
  120.1 1.8 collective-permute-start.13
  121.9 1.3 collective-permute-start.17
  123.2 6.2 %fusion.7 = (f32[2560,128]{1,0:T(8,128)}, f32[2560,128]{1,0:T(8,128)}) fusion(s32[2560,128]{1,0:T(8,128)S(1)} %copy-done.5, s32[]{:T(128)} %bitcast.10), kind=kLoop, calls=%fused_computation.18 | loop fusion | flops 4587520 | bytes 3932164 | tf_op jit(solution)/shard_map/cos | solution.py:337
  129.4 3.9 %collective-permute-start.15 = (bf16[128,2048]{1,0:T(8,128)(2,1)}, bf16[128,2048]{1,0:T(8,128)(2,1)}, u32[]{:S(2)}, u32[]{:S(2)}) collective-permute-start(bf16[128,2048]{1,0:T(8,128)(2,1)} %select_select_fusion.refs_0_), channel_id=1, source_target_pairs={{0,4},{2,6},{4,0},{6,2},{8,12},{10,14},{12,8},{14,10},{16,20},{18,... | collective-permute-start | bytes 1572872 | tf_op jit(solution)/shard_map/ppermute | solution.py:342
  133.3 0.0 collective-permute-start.14
  133.3 2.0 all-to-all-done
  135.3 4.3 %all-to-all-start.1 = ((bf16[4,64,2048]{2,1,0:T(8,128)(2,1)}), bf16[4,64,2048]{2,1,0:T(8,128)(2,1)}, u32[]{:S(2)}, u32[]{:S(2)}) async-start(bf16[4,64,2048]{2,1,0:T(8,128)(2,1)} %bitcast.4), calls=%async_computation.1 | async-start | bytes 2097152 | tf_op jit(solution)/shard_map/all_to_all | solution.py:388
  139.6 3.4 pad_maximum_fusion.steer_ref
  143.0 0.7 slice.32
  143.7 0.8 dynamic_slice.3
  144.5 0.6 reshape.21.refs_6_
  145.1 0.6 pad_add_fusion.spot_ref
  145.7 2.1 fusion.9
  147.7 0.8 pad_maximum_fusion.1.top_ref
  148.6 1.5 collective-permute-done.16.refs_3_
  150.1 13.3 %collective-permute-done.15.refs_2_ = bf16[128,2048]{1,0:T(8,128)(2,1)} collective-permute-done((bf16[128,2048]{1,0:T(8,128)(2,1)}, bf16[128,2048]{1,0:T(8,128)(2,1)}, u32[]{:S(2)}, u32[]{:S(2)}) %collective-permute-start.15) | collective-permute-done | bytes 524320 | tf_op jit(solution)/shard_map/ppermute | solution.py:342
  163.4 13.9 %collective-permute-done.17.refs_5_ = bf16[384,2048]{1,0:T(8,128)(2,1)} collective-permute-done((bf16[384,2048]{1,0:T(8,128)(2,1)}, bf16[384,2048]{1,0:T(8,128)(2,1)}, u32[]{:S(2)}, u32[]{:S(2)}) %collective-permute-start.17) | collective-permute-done | bytes 1572896 | tf_op jit(solution)/shard_map/ppermute | solution.py:342
  177.3 2.3 shard_map.67
  179.6 0.0 copy-start
  179.6 2.7 copy-done
  182.3 5.2 %all-to-all-start.2 = ((bf16[4,384,2048]{2,1,0:T(8,128)(2,1)}), bf16[4,384,2048]{2,1,0:T(8,128)(2,1)}, u32[]{:S(2)}, u32[]{:S(2)}) async-start(bf16[4,384,2048]{2,1,0:T(8,128)(2,1)} %bitcast.12), calls=%async_computation.2 | async-start | bytes 12582912 | tf_op jit(solution)/shard_map/all_to_all | solution.py:391
  187.5 0.2 all-gather.3.cloned.1.call-start
  187.7 0.5 all-gather.3.cloned.1.call-update
  188.3 41.0 %shard_map.68 = (f32[512,512]{1,0:T(8,128)S(1)}, bf16[512,2048]{1,0:T(8,128)(2,1)S(1)}) custom-call(s32[1]{0:T(128)} %bitcast.1.spot_ref, bf16[128,2048]{1,0:T(8,128)(2,1)} %select_select_fusion.refs_0_, bf16[128,2048]{1,0:T(8,128)(2,1)} %collective-permute-done.14.refs_1_, bf16[128,2048]{1,0:T(8,128)(2,1)} %collective-permute-done.15.refs_2_, ...), custom_call_target="tpu_custom_call" | custom-call | flops 40000000000 | bytes 4000000 | tf_op jit(solution)/shard_map/pallas_call | solution.py:110
  229.3 0.0 all-gather.5.cloned.1.call-done.rows_ref.refs_1_
  229.3 0.0 copy-start.3
  229.3 1.4 copy-done.3
  230.7 22.2 %shard_map.69 = (f32[2560,512]{1,0:T(8,128)}, bf16[2560,512]{1,0:T(8,128)(2,1)}, bf16[2560,512]{1,0:T(8,128)(2,1)}, f32[2,2560,128]{2,1,0:T(8,128)}) custom-call(s32[1]{0:T(128)} %bitcast.spot_ref, bf16[2560,2048]{1,0:T(8,128)(2,1)} %all-gather.5.cloned.1.call-done.rows_ref.refs_1_, bf16[512,2048]{1,0:T(8,128)(2,1)S(1)} %get-tuple-element.41.head_ref.refs_4_, ...), custom_call_target="tpu_custom_call" | custom-call | flops 13421772800 | bytes 20971520 | tf_op jit(solution)/shard_map/pallas_call | solution.py:158
  253.0 46.4 %shard_map.70.refs_7_ = f32[2560,2560]{1,0:T(8,128)} custom-call(s32[2]{0:T(128)} %pad_add_fusion.spot_ref, bf16[1536,2048]{1,0:T(8,128)(2,1)} %bitcast.9.refs_0_, bf16[2560,2048]{1,0:T(8,128)(2,1)} %all-gather.5.cloned.1.call-done.rows_ref.refs_1_, bf16[2560,512]{1,0:T(8,128)(2,1)} %get-tuple-element.43.refs_2_, ...), custom_call_target="tpu_custom_call" | custom-call | flops 28185722880 | bytes 26214400 | tf_op jit(solution)/shard_map/pallas_call | solution.py:264
  299.4 0.0 all-gather.3.cloned.1.call-done.refs_0_
  299.4 33.5 %shard_map.71 = f32[2560,2560]{1,0:T(8,128)} custom-call(s32[2]{0:T(128)} %pad_add_fusion.spot_ref, bf16[1024,2048]{1,0:T(8,128)(2,1)} %all-gather.3.cloned.1.call-done.refs_0_, bf16[2560,2048]{1,0:T(8,128)(2,1)} %all-gather.5.cloned.1.call-done.rows_ref.refs_1_, bf16[2560,512]{1,0:T(8,128)(2,1)} %get-tuple-element.43.refs_2_, ...), custom_call_target="tpu_custom_call", output_to_operand_aliasing={{}: (8, {})} | custom-call | flops 18790481920 | bytes 20971520 | tf_op jit(solution)/shard_map/pallas_call | solution.py:264
  (15 shorter events, 0.0 us)
Async XLA Ops:
  7.2 222.1 %all-gather.5.cloned.1.call-start = ((), (), s32[]{:S(2)}) async-start(), calls=%async_computation.4 | async-start | bytes 13107200 | tf_op jit(solution)/shard_map/all_gather | solution.py:374
  7.9 9.8 %copy-start.4 = (bf16[640,2048]{1,0:T(8,128)(2,1)S(1)}, bf16[640,2048]{1,0:T(8,128)(2,1)}, u32[]{:S(2)}) copy-start(bf16[640,2048]{1,0:T(8,128)(2,1)} %param.4) | copy-start | bytes 7864324
  9.6 63.4 %collective-permute-start.4 = (bf16[384,2048]{1,0:T(8,128)(2,1)S(1)}, bf16[384,2048]{1,0:T(8,128)(2,1)S(1)}, u32[]{:S(2)}, u32[]{:S(2)}) collective-permute-start(bf16[384,2048]{1,0:T(8,128)(2,1)S(1)} %slice.30.own), channel_id=1, source_target_pairs={{8,0},{10,2},{12,4},{14,6},{16,8},{18,10},{20,12},{22,14},{24,16},... | collective-permute-start | bytes 4718600 | tf_op jit(solution)/shard_map/ppermute | solution.py:342
  10.9 62.1 %collective-permute-start.3 = (bf16[384,2048]{1,0:T(8,128)(2,1)S(1)}, bf16[384,2048]{1,0:T(8,128)(2,1)}, u32[]{:S(2)}, u32[]{:S(2)}) collective-permute-start(bf16[384,2048]{1,0:T(8,128)(2,1)S(1)} %slice.30.own), channel_id=1, source_target_pairs={{0,8},{2,10},{4,12},{6,14},{8,16},{10,18},{12,20},{14,22},{16,24},... | collective-permute-start | bytes 4718600 | tf_op jit(solution)/shard_map/ppermute | solution.py:342
  18.8 28.6 %collective-permute-start.2 = (bf16[128,2048]{1,0:T(8,128)(2,1)}, bf16[128,2048]{1,0:T(8,128)(2,1)}, u32[]{:S(2)}, u32[]{:S(2)}) collective-permute-start(bf16[128,2048]{1,0:T(8,128)(2,1)} %get-tuple-element.47), channel_id=1, source_target_pairs={{0,6},{1,7}} | collective-permute-start | bytes 1572872 | tf_op jit(solution)/shard_map/ppermute | solution.py:342
  24.4 24.5 %collective-permute-start.1 = (bf16[128,2048]{1,0:T(8,128)(2,1)}, bf16[128,2048]{1,0:T(8,128)(2,1)}, u32[]{:S(2)}, u32[]{:S(2)}) collective-permute-start(bf16[128,2048]{1,0:T(8,128)(2,1)} %get-tuple-element.48), channel_id=1, source_target_pairs={{0,4},{1,5}} | collective-permute-start | bytes 1572872 | tf_op jit(solution)/shard_map/ppermute | solution.py:342
  26.5 42.7 %collective-permute-start = (bf16[128,2048]{1,0:T(8,128)(2,1)}, bf16[128,2048]{1,0:T(8,128)(2,1)}, u32[]{:S(2)}, u32[]{:S(2)}) collective-permute-start(bf16[128,2048]{1,0:T(8,128)(2,1)} %get-tuple-element.49), channel_id=1, source_target_pairs={{0,2},{1,3}} | collective-permute-start | bytes 1572872 | tf_op jit(solution)/shard_map/ppermute | solution.py:342
  47.4 25.2 %collective-permute-start.7 = (s16[512,128]{1,0:T(8,128)(2,1)S(1)}, s16[512,128]{1,0:T(8,128)(2,1)S(1)}, u32[]{:S(2)}, u32[]{:S(2)}) collective-permute-start(s16[512,128]{1,0:T(8,128)(2,1)S(1)} %slice_convert_fusion), channel_id=1, source_target_pairs={{0,24},{2,26},{4,28},{6,30},{1,25},{3,27},{5,29},{7,31}} | collective-permute-start | bytes 393224 | tf_op jit(solution)/shard_map/ppermute | solution.py:342
  49.0 23.7 %collective-permute-start.6 = (s16[512,128]{1,0:T(8,128)(2,1)S(1)}, s16[512,128]{1,0:T(8,128)(2,1)S(1)}, u32[]{:S(2)}, u32[]{:S(2)}) collective-permute-start(s16[512,128]{1,0:T(8,128)(2,1)S(1)} %slice_convert_fusion), channel_id=1, source_target_pairs={{0,16},{2,18},{4,20},{6,22},{1,17},{3,19},{5,21},{7,23}} | collective-permute-start | bytes 393224 | tf_op jit(solution)/shard_map/ppermute | solution.py:342
  69.2 3.8 %collective-permute-start.5 = (s16[512,128]{1,0:T(8,128)(2,1)S(1)}, s16[512,128]{1,0:T(8,128)(2,1)S(1)}, u32[]{:S(2)}, u32[]{:S(2)}) collective-permute-start(s16[512,128]{1,0:T(8,128)(2,1)S(1)} %slice_convert_fusion), channel_id=1, source_target_pairs={{0,8},{2,10},{4,12},{6,14},{1,9},{3,11},{5,13},{7,15}} | collective-permute-start | bytes 393224 | tf_op jit(solution)/shard_map/ppermute | solution.py:342
  73.0 41.7 %collective-permute-start.11 = (bf16[384,2048]{1,0:T(8,128)(2,1)}, bf16[384,2048]{1,0:T(8,128)(2,1)}, u32[]{:S(2)}, u32[]{:S(2)}) collective-permute-start(bf16[384,2048]{1,0:T(8,128)(2,1)} %collective-permute-done.3.refs_0_), channel_id=1, source_target_pairs={{8,16},{10,18},{12,20},{14,22},{16,24},{18,26},{20,28},{22,30},{9,... | collective-permute-start | bytes 4718600 | tf_op jit(solution)/shard_map/ppermute | solution.py:342
  74.9 45.3 %collective-permute-start.12 = (bf16[384,2048]{1,0:T(8,128)(2,1)S(1)}, bf16[384,2048]{1,0:T(8,128)(2,1)}, u32[]{:S(2)}, u32[]{:S(2)}) collective-permute-start(bf16[384,2048]{1,0:T(8,128)(2,1)S(1)} %collective-permute-done.4.refs_3_), channel_id=1, source_target_pairs={{8,0},{10,2},{12,4},{14,6},{16,8},{18,10},{20,12},{22,14},{9,1},{1... | collective-permute-start | bytes 4718600 | tf_op jit(solution)/shard_map/ppermute | solution.py:342
  76.1 19.9 %collective-permute-start.10 = (bf16[128,2048]{1,0:T(8,128)(2,1)}, bf16[128,2048]{1,0:T(8,128)(2,1)}, u32[]{:S(2)}, u32[]{:S(2)}) collective-permute-start(bf16[128,2048]{1,0:T(8,128)(2,1)} %select_select_fusion.1), channel_id=1, source_target_pairs={{0,24},{2,26},{4,28},{6,30},{1,25},{3,27},{5,29},{7,31}} | collective-permute-start | bytes 1572872 | tf_op jit(solution)/shard_map/ppermute | solution.py:342
  78.3 23.1 %collective-permute-start.9 = (bf16[128,2048]{1,0:T(8,128)(2,1)}, bf16[128,2048]{1,0:T(8,128)(2,1)}, u32[]{:S(2)}, u32[]{:S(2)}) collective-permute-start(bf16[128,2048]{1,0:T(8,128)(2,1)} %select_select_fusion.1), channel_id=1, source_target_pairs={{0,16},{2,18},{4,20},{6,22},{1,17},{3,19},{5,21},{7,23}} | collective-permute-start | bytes 1572872 | tf_op jit(solution)/shard_map/ppermute | solution.py:342
  86.6 26.0 %collective-permute-start.8 = (bf16[128,2048]{1,0:T(8,128)(2,1)}, bf16[128,2048]{1,0:T(8,128)(2,1)}, u32[]{:S(2)}, u32[]{:S(2)}) collective-permute-start(bf16[128,2048]{1,0:T(8,128)(2,1)} %select_select_fusion.1), channel_id=1, source_target_pairs={{0,8},{2,10},{4,12},{6,14},{1,9},{3,11},{5,13},{7,15}} | collective-permute-start | bytes 1572872 | tf_op jit(solution)/shard_map/ppermute | solution.py:342
  91.0 44.3 %all-to-all-start = ((bf16[4,64,2048]{2,1,0:T(8,128)(2,1)}), bf16[4,64,2048]{2,1,0:T(8,128)(2,1)}, u32[]{:S(2)}, u32[]{:S(2)}) async-start(bf16[4,64,2048]{2,1,0:T(8,128)(2,1)} %bitcast.15), calls=%async_computation | async-start | bytes 2097152 | tf_op jit(solution)/shard_map/all_to_all | solution.py:383
  95.3 27.9 %copy-start.5 = (s32[2560,128]{1,0:T(8,128)S(1)}, s32[2560,128]{1,0:T(8,128)}, u32[]{:S(2)}) copy-start(s32[2560,128]{1,0:T(8,128)} %param.6) | copy-start | bytes 3932164
  120.1 43.3 %collective-permute-start.13 = (bf16[384,2048]{1,0:T(8,128)(2,1)}, bf16[384,2048]{1,0:T(8,128)(2,1)}, u32[]{:S(2)}, u32[]{:S(2)}) collective-permute-start(bf16[384,2048]{1,0:T(8,128)(2,1)} %collective-permute-done.11.refs_1_), channel_id=1, source_target_pairs={{16,24},{18,26},{20,28},{22,30},{17,25},{19,27},{21,29},{23,31}} | collective-permute-start | bytes 4718600 | tf_op jit(solution)/shard_map/ppermute | solution.py:342
  121.9 55.4 %collective-permute-start.17 = (bf16[384,2048]{1,0:T(8,128)(2,1)}, bf16[384,2048]{1,0:T(8,128)(2,1)}, u32[]{:S(2)}, u32[]{:S(2)}) collective-permute-start(bf16[384,2048]{1,0:T(8,128)(2,1)} %collective-permute-done.12.refs_4_), channel_id=1, source_target_pairs={{8,0},{10,2},{12,4},{14,6},{9,1},{11,3},{13,5},{15,7}} | collective-permute-start | bytes 4718600 | tf_op jit(solution)/shard_map/ppermute | solution.py:342
  129.4 20.7 %collective-permute-start.16 = (bf16[128,2048]{1,0:T(8,128)(2,1)}, bf16[128,2048]{1,0:T(8,128)(2,1)}, u32[]{:S(2)}, u32[]{:S(2)}) collective-permute-start(bf16[128,2048]{1,0:T(8,128)(2,1)} %select_select_fusion.refs_0_), channel_id=1, source_target_pairs={{0,6},{2,4},{4,2},{6,0},{8,14},{10,12},{12,10},{14,8},{16,22},{18,... | collective-permute-start | bytes 1572872 | tf_op jit(solution)/shard_map/ppermute | solution.py:342
  129.4 34.0 %collective-permute-start.15 = (bf16[128,2048]{1,0:T(8,128)(2,1)}, bf16[128,2048]{1,0:T(8,128)(2,1)}, u32[]{:S(2)}, u32[]{:S(2)}) collective-permute-start(bf16[128,2048]{1,0:T(8,128)(2,1)} %select_select_fusion.refs_0_), channel_id=1, source_target_pairs={{0,4},{2,6},{4,0},{6,2},{8,12},{10,14},{12,8},{14,10},{16,20},{18,... | collective-permute-start | bytes 1572872 | tf_op jit(solution)/shard_map/ppermute | solution.py:342
  133.3 30.0 %collective-permute-start.14 = (bf16[128,2048]{1,0:T(8,128)(2,1)}, bf16[128,2048]{1,0:T(8,128)(2,1)}, u32[]{:S(2)}, u32[]{:S(2)}) collective-permute-start(bf16[128,2048]{1,0:T(8,128)(2,1)} %select_select_fusion.refs_0_), channel_id=1, source_target_pairs={{0,2},{2,0},{4,6},{6,4},{8,10},{10,8},{12,14},{14,12},{16,18},{18,... | collective-permute-start | bytes 1572872 | tf_op jit(solution)/shard_map/ppermute | solution.py:342
  135.3 46.9 %all-to-all-start.1 = ((bf16[4,64,2048]{2,1,0:T(8,128)(2,1)}), bf16[4,64,2048]{2,1,0:T(8,128)(2,1)}, u32[]{:S(2)}, u32[]{:S(2)}) async-start(bf16[4,64,2048]{2,1,0:T(8,128)(2,1)} %bitcast.4), calls=%async_computation.1 | async-start | bytes 2097152 | tf_op jit(solution)/shard_map/all_to_all | solution.py:388
  179.6 2.7 copy-start
  182.3 70.7 %all-to-all-start.2 = ((bf16[4,384,2048]{2,1,0:T(8,128)(2,1)}), bf16[4,384,2048]{2,1,0:T(8,128)(2,1)}, u32[]{:S(2)}, u32[]{:S(2)}) async-start(bf16[4,384,2048]{2,1,0:T(8,128)(2,1)} %bitcast.12), calls=%async_computation.2 | async-start | bytes 12582912 | tf_op jit(solution)/shard_map/all_to_all | solution.py:391
  187.5 111.9 %all-gather.3.cloned.1.call-start = ((), (), s32[]{:S(2)}) async-start(), calls=%async_computation.3 | async-start | bytes 5242880 | tf_op jit(solution)/shard_map/all_gather | solution.py:392
  229.3 23.7 %copy-start.1 = (bf16[512,2048]{1,0:T(8,128)(2,1)}, bf16[512,2048]{1,0:T(8,128)(2,1)S(1)}, u32[]{:S(2)}) copy-start(bf16[512,2048]{1,0:T(8,128)(2,1)S(1)} %get-tuple-element.41.head_ref.refs_4_) | copy-start | bytes 6291460
  229.3 23.7 %copy-start.2 = (f32[512,512]{1,0:T(8,128)}, f32[512,512]{1,0:T(8,128)S(1)}, u32[]{:S(2)}) copy-start(f32[512,512]{1,0:T(8,128)S(1)} %get-tuple-element.42.inv_ref.refs_5_) | copy-start | bytes 3145732
  229.3 1.4 copy-start.3
Sparse Core Ops, SparseCore 0:
  9.8 143.6 all-gather.4
  189.9 86.5 all-gather.2

commit v3 on v2

--- a/solution.py
+++ b/solution.py
@@ -10,7 +10,7 @@
 PANEL = 512
 NFFT = 2048
 BLK = 128
-SUB = 8
+SUB = 16
 
 two_pi = 6.283185307179586
 F32 = jnp.float32
@@ -88,20 +88,15 @@
     gram = dot_nt(head_ref[...], head_ref[...]) / snap
     csd[...] = gram + jnp.where(row == col, load_ref[...], 0.0)
     inv_ref[...] = jnp.where(row == col, 1.0, 0.0)
-    below = lax.broadcasted_iota(jnp.int32, (n, BLK), 0)
-
-    def step(k, _):
-        at = pl.multiple_of(k * BLK, BLK)
-        inv = inverse_factor(csd[pl.ds(at, BLK), pl.ds(at, BLK)])
-        side = dot_nt(csd[:, pl.ds(at, BLK)], inv, HIGHEST)
-        side = jnp.where(below >= at + BLK, side, 0.0)
-        own = jnp.dot(inv, inv_ref[pl.ds(at, BLK), :], precision=HIGHEST, preferred_element_type=F32)
-        inv_ref[pl.ds(at, BLK), :] = own
-        inv_ref[...] -= jnp.dot(side, own, precision=HIGHEST, preferred_element_type=F32)
-        csd[...] -= dot_nt(side, side, HIGHEST)
-        return 0
-
-    lax.fori_loop(0, n // BLK, step, 0)
+    for at in range(0, n, BLK):
+        end = at + BLK
+        inv = inverse_factor(csd[at:end, at:end])
+        own = jnp.dot(inv, inv_ref[at:end, :end], precision=HIGHEST, preferred_element_type=F32)
+        inv_ref[at:end, :end] = own
+        if end < n:
+            side = dot_nt(csd[end:, at:end], inv, HIGHEST)
+            csd[end:, end:] -= dot_nt(side, side, HIGHEST)
+            inv_ref[end:, :end] -= jnp.dot(side, own, precision=HIGHEST, preferred_element_type=F32)
 
 
 def head_factor(spot, pieces, load, snap):
@@ -328,13 +323,13 @@
     )(spot, own, *ups, *downs)
 
 
-def after(value, *others):
-    return lax.optimization_barrier((value, *others))[0]
-
-
 def steer_of(delays, bin_index):
     angle = (delays * bin_index % NFFT).astype(F32) * (two_pi / NFFT)
     return jnp.concatenate([jnp.cos(angle), jnp.sin(angle)], axis=1)
+
+
+def after(value, *others):
+    return lax.optimization_barrier((value, *others))[0]
 
 
 def planned(count):
@@ -374,29 +369,29 @@
         own_rows = lax.all_gather(spectra, "col", axis=0, tiled=True)
         one = hop([first, first], 1)
         held = chosen(col, [quarters[0]] + [move(quarters[j], [((0, 0), (0, j))]) for j in range(1, count)])
-        top = delays[:PANEL].astype(jnp.int16)
+        rest = lax.all_to_all(after(spectra[early:], held), "row", 0, 0, tiled=True)
+
+        two = hop(one, 2)
+        top = after(delays[:PANEL].astype(jnp.int16), *one)
         tops = [top] + [move(top, [((0, p), (k, p)) for p in range(count)]) for k in range(1, count)]
-
-        held = after(held, *one, *tops)
+        held = after(held, *two, *tops, rest)
+        rest = lax.all_to_all(rest, "col", 0, 0, tiled=True)
+
         lifted = [held] + [move(held, [((0, p), (k, p)) for p in range(count)]) for k in range(1, count)]
-        two = hop([after(v, held) for v in one], 2)
-        rest = lax.all_to_all(after(spectra[early:], held), "row", 0, 0, tiled=True)
-        piece = after(chosen(row, lifted), *two)
-
-        pieces = [piece] + [move(piece, across(m)) for m in range(1, count)]
-        three = hop([after(v, piece) for v in two], 3)
-        rest = lax.all_to_all(after(rest, piece), "col", 0, 0, tiled=True)
-        three = [after(v, *pieces) for v in three]
+        three = hop([after(v, held) for v in two], 3)
+        piece = after(chosen(row, lifted), rest, *tops, *three)
+
         stacked = in_line(spot_row, first, [one[0], two[0], three[0]], [one[1], two[1], three[1]])
         cols_first = lax.all_to_all(stacked, "col", 0, 0, tiled=True)
-        cols_rest = lax.all_gather(after(rest, stacked), "row", axis=0, tiled=True)
+        cols_rest = lax.all_gather(rest, "row", axis=0, tiled=True)
+        pieces = [piece] + [move(piece, across(m)) for m in range(1, count)]
 
         pieces = [after(v, stacked) for v in pieces]
         inv, head = head_factor(col.astype(jnp.int32).reshape(1), pieces, head_load, snap)
         steer_top = steer_of(chosen(row, tops).astype(jnp.int32), bin_index[0])
         steer = steer_of(delays, bin_index[0])
         panel, high, low, whitened = own_panel(
-            spot_row, after(own_rows, rest), head, inv, head_load, steer, steer_top, snap, PANEL
+            spot_row, own_rows, head, inv, head_load, steer, steer_top, snap, PANEL
         )
 
         load = lax.dynamic_slice_in_dim(loading, col * size, size).reshape(1, size)

time: 347 us -> 344 us (level)
  Pallas kernels: 145 us -> 126 us
  starting transfers between devices: 58.4 us -> 68.5 us
  waiting for transfers between devices: 91.3 us -> 98.4 us
    pallas_call x1, Pallas kernels: 41 us -> 21.7 us  [head_factor(): pl.pallas_call(functools.partial(factor_kernel, snap, len(pieces)), out_s...]
    all_to_all x1, waiting for transfers between devices: 0.01 us -> 18.5 us  [on_device(): cols_first = lax.all_to_all(stacked, 'col', 0, 0, tiled=True)]
    ppermute x18, waiting for transfers between devices: 88.1 us -> 73.2 us  [move(): lax.ppermute(value, ('row', 'col'), [(a * count + b, c * count + d) for (...]
    ppermute x18, starting transfers between devices: 44.4 us -> 54.3 us  [move(): lax.ppermute(value, ('row', 'col'), [(a * count + b, c * count + d) for (...]
    all_to_all x1, waiting for transfers between devices: 1.99 us -> 6.08 us  [on_device(): rest = lax.all_to_all(after(spectra[early:], held), 'row', 0, 0, tiled=True)]
  transfers between devices with their start and end apart: 23 -> 23, of which waited for: 11 -> 11; matrix products, arithmetic and copies ran while one was open for 8% -> 7% of each run, Pallas kernels for 33% -> 27%
where the time goes in v3:
time: 344 us; the launch traced here: 339 us
  Pallas kernels  126 us (37%)
  waiting for transfers between devices  98.4 us (29%)
  starting transfers between devices  68.5 us (20%)
  other arithmetic  19.2 us (6%)
  between operations  15.4 us (4%)
  local copies, waits for them, and re-layouts  11.9 us (3%)
    pallas_call x2, Pallas kernels, trailing_part(): pl.pallas_call(functools.partial(trailing_kernel, snap, geo, gather), gri...  79.6 us
    ppermute x18, waiting for transfers between devices, move(): lax.ppermute(value, ('row', 'col'), [(a * count + b, c * count + d) for (...  73.2 us
    ppermute x18, starting transfers between devices, move(): lax.ppermute(value, ('row', 'col'), [(a * count + b, c * count + d) for (...  54.3 us
    pallas_call x1, Pallas kernels, own_panel(): pl.pallas_call(functools.partial(panel_kernel, snap), grid=(n // tile,),...  22.5 us
    pallas_call x1, Pallas kernels, head_factor(): pl.pallas_call(functools.partial(factor_kernel, snap, len(pieces)), out_s...  21.7 us
    all_to_all x1, waiting for transfers between devices, on_device(): cols_first = lax.all_to_all(stacked, 'col', 0, 0, tiled=True)  18.5 us
    cos x2, other arithmetic, steer_of(): return jnp.concatenate([jnp.cos(angle), jnp.sin(angle)], axis=1)  9.28 us
  transfers between devices with their start and end apart: 23, of which 11 were waited for; matrix products, arithmetic and copies ran while one was open for 7% of the time, Pallas kernels for 27%

profile of v3, /device:TPU:0, one launch (start us, length us, event | category | flops | bytes accessed | tf_op | source)
XLA Modules:
  0.0 339.4 jit_solution(12486796701754324988)
XLA Ops:
  7.2 0.0 all-gather.5.cloned.1.call-start
  7.2 0.7 all-gather.5.cloned.1.call-update
  7.9 0.0 copy-start.5
  7.9 1.7 slice.30.own
  9.6 1.3 collective-permute-start.5
  10.9 6.7 %collective-permute-start.3 = (bf16[384,2048]{1,0:T(8,128)(2,1)S(1)}, bf16[384,2048]{1,0:T(8,128)(2,1)}, u32[]{:S(2)}, u32[]{:S(2)}) collective-permute-start(bf16[384,2048]{1,0:T(8,128)(2,1)S(1)} %slice.30.own), channel_id=1, source_target_pairs={{0,8},{2,10},{4,12},{6,14},{8,16},{10,18},{12,20},{14,22},{16,24},... | collective-permute-start | bytes 4718600 | tf_op jit(solution)/shard_map/ppermute | solution.py:337
  17.7 1.2 fusion.10
  18.9 5.6 %collective-permute-start.2 = (bf16[128,2048]{1,0:T(8,128)(2,1)}, bf16[128,2048]{1,0:T(8,128)(2,1)}, u32[]{:S(2)}, u32[]{:S(2)}) collective-permute-start(bf16[128,2048]{1,0:T(8,128)(2,1)} %get-tuple-element.35), channel_id=1, source_target_pairs={{0,6},{1,7}} | collective-permute-start | bytes 1572872 | tf_op jit(solution)/shard_map/ppermute | solution.py:337
  24.4 2.1 collective-permute-start.1
  26.5 2.1 collective-permute-start
  28.6 1.0 slice.25
  29.7 19.3 %collective-permute-done.5.refs_3_ = bf16[384,2048]{1,0:T(8,128)(2,1)S(1)} collective-permute-done((bf16[384,2048]{1,0:T(8,128)(2,1)S(1)}, bf16[384,2048]{1,0:T(8,128)(2,1)S(1)}, u32[]{:S(2)}, u32[]{:S(2)}) %collective-permute-start.5) | collective-permute-done | bytes 1572896 | tf_op jit(solution)/shard_map/ppermute | solution.py:337
  49.0 1.3 collective-permute-start.6
  50.3 1.8 collective-permute-start.4
  52.1 17.1 %collective-permute-done = bf16[128,2048]{1,0:T(8,128)(2,1)} collective-permute-done((bf16[128,2048]{1,0:T(8,128)(2,1)}, bf16[128,2048]{1,0:T(8,128)(2,1)}, u32[]{:S(2)}, u32[]{:S(2)}) %collective-permute-start) | collective-permute-done | bytes 524320 | tf_op jit(solution)/shard_map/ppermute | solution.py:337
  69.2 2.1 select_select_fusion.1
  71.3 4.3 %all-to-all-start = ((bf16[4,64,2048]{2,1,0:T(8,128)(2,1)}), bf16[4,64,2048]{2,1,0:T(8,128)(2,1)}, u32[]{:S(2)}, u32[]{:S(2)}) async-start(bf16[4,64,2048]{2,1,0:T(8,128)(2,1)} %bitcast.13), calls=%async_computation | async-start | bytes 2097152 | tf_op jit(solution)/shard_map/all_to_all | solution.py:372
  75.6 1.0 slice_convert_fusion
  76.6 5.7 %collective-permute-start.9 = (s16[512,128]{1,0:T(8,128)(2,1)S(1)}, s16[512,128]{1,0:T(8,128)(2,1)S(1)}, u32[]{:S(2)}, u32[]{:S(2)}) collective-permute-start(s16[512,128]{1,0:T(8,128)(2,1)S(1)} %slice_convert_fusion), channel_id=1, source_target_pairs={{0,24},{2,26},{4,28},{6,30},{1,25},{3,27},{5,29},{7,31}} | collective-permute-start | bytes 393224 | tf_op jit(solution)/shard_map/ppermute | solution.py:337
  82.3 1.3 collective-permute-start.8
  83.6 1.3 collective-permute-start.7
  84.9 11.8 %collective-permute-done.9 = s16[512,128]{1,0:T(8,128)(2,1)S(1)} collective-permute-done((s16[512,128]{1,0:T(8,128)(2,1)S(1)}, s16[512,128]{1,0:T(8,128)(2,1)S(1)}, u32[]{:S(2)}, u32[]{:S(2)}) %collective-permute-start.9) | collective-permute-done | bytes 131104 | tf_op jit(solution)/shard_map/ppermute | solution.py:337
  96.6 1.5 collective-permute-done.8
  98.1 1.4 collective-permute-done.7
  99.5 0.6 copy-done.6
  100.2 1.8 collective-permute-start.13
  102.0 1.3 collective-permute-start.14
  103.9 6.1 %all-to-all-done = bf16[4,64,2048]{2,1,0:T(8,128)(2,1)} async-done(((bf16[4,64,2048]{2,1,0:T(8,128)(2,1)}), bf16[4,64,2048]{2,1,0:T(8,128)(2,1)}, u32[]{:S(2)}, u32[]{:S(2)}) %all-to-all-start) | async-done | bytes 1048608 | tf_op jit(solution)/shard_map/all_to_all | solution.py:372
  110.0 4.2 %all-to-all-start.1 = ((bf16[4,64,2048]{2,1,0:T(8,128)(2,1)}), bf16[4,64,2048]{2,1,0:T(8,128)(2,1)}, u32[]{:S(2)}, u32[]{:S(2)}) async-start(bf16[4,64,2048]{2,1,0:T(8,128)(2,1)} %all-to-all-done), calls=%async_computation.1 | async-start | bytes 2097152 | tf_op jit(solution)/shard_map/all_to_all | solution.py:378
  114.3 0.0 all-gather.3.cloned.1.call-start
  114.3 14.3 %collective-permute-start.12 = (bf16[128,2048]{1,0:T(8,128)(2,1)}, bf16[128,2048]{1,0:T(8,128)(2,1)}, u32[]{:S(2)}, u32[]{:S(2)}) collective-permute-start(bf16[128,2048]{1,0:T(8,128)(2,1)} %select_select_fusion.1), channel_id=1, source_target_pairs={{0,24},{2,26},{4,28},{6,30},{1,25},{3,27},{5,29},{7,31}} | collective-permute-start | bytes 1572872 | tf_op jit(solution)/shard_map/ppermute | solution.py:337
  128.6 2.1 collective-permute-start.11
  130.7 2.1 collective-permute-start.10
  132.8 8.1 %fusion.7 = (f32[2560,128]{1,0:T(8,128)}, f32[2560,128]{1,0:T(8,128)}) fusion(s32[2560,128]{1,0:T(8,128)} %param.6, s32[]{:T(128)} %bitcast.8), kind=kLoop, calls=%fused_computation.18 | loop fusion | flops 4587520 | bytes 3932164 | tf_op jit(solution)/shard_map/cos | solution.py:328
  140.9 10.8 %collective-permute-done.11 = bf16[128,2048]{1,0:T(8,128)(2,1)} collective-permute-done((bf16[128,2048]{1,0:T(8,128)(2,1)}, bf16[128,2048]{1,0:T(8,128)(2,1)}, u32[]{:S(2)}, u32[]{:S(2)}) %collective-permute-start.11) | collective-permute-done | bytes 524320 | tf_op jit(solution)/shard_map/ppermute | solution.py:337
  151.7 8.0 %collective-permute-done.10 = bf16[128,2048]{1,0:T(8,128)(2,1)} collective-permute-done((bf16[128,2048]{1,0:T(8,128)(2,1)}, bf16[128,2048]{1,0:T(8,128)(2,1)}, u32[]{:S(2)}, u32[]{:S(2)}) %collective-permute-start.10) | collective-permute-done | bytes 524320 | tf_op jit(solution)/shard_map/ppermute | solution.py:337
  159.7 2.1 select_select_fusion.refs_0_
  161.8 2.6 collective-permute-start.17
  164.4 0.6 collective-permute-start.16
  165.0 0.4 collective-permute-start.15
  165.4 3.4 pad_maximum_fusion.steer_ref
  168.8 0.7 slice.32
  169.4 0.8 dynamic_slice.3
  170.2 0.6 reshape.22.refs_6_
  170.8 0.6 pad_add_fusion.spot_ref
  171.4 1.2 fusion.9
  172.6 0.8 pad_maximum_fusion.1.top_ref
  173.4 0.0 all-gather.3.cloned.1.call-update
  173.5 2.3 shard_map.67
  175.7 0.0 copy-start
  175.8 2.7 copy-done
  178.5 5.6 %all-to-all-start.2 = ((bf16[4,384,2048]{2,1,0:T(8,128)(2,1)}), bf16[4,384,2048]{2,1,0:T(8,128)(2,1)}, u32[]{:S(2)}, u32[]{:S(2)}) async-start(bf16[4,384,2048]{2,1,0:T(8,128)(2,1)} %bitcast.10), calls=%async_computation.2 | async-start | bytes 12582912 | tf_op jit(solution)/shard_map/all_to_all | solution.py:385
  184.0 2.4 collective-permute-done.16.refs_2_
  186.5 0.8 collective-permute-done.15.refs_1_
  187.3 1.0 copy-done.4
  188.3 21.7 %shard_map.68 = (f32[512,512]{1,0:T(8,128)S(1)}, bf16[512,2048]{1,0:T(8,128)(2,1)S(1)}) custom-call(s32[1]{0:T(128)} %bitcast.1.spot_ref, bf16[128,2048]{1,0:T(8,128)(2,1)S(1)} %copy-done.4, bf16[128,2048]{1,0:T(8,128)(2,1)} %collective-permute-done.15.refs_1_, bf16[128,2048]{1,0:T(8,128)(2,1)} %collective-permute-done.16.refs_2_, ...), custom_call_target="tpu_custom_call" | custom-call | flops 40000000000 | bytes 4000000 | tf_op jit(solution)/shard_map/pallas_call | solution.py:105
  210.0 0.0 all-gather.5.cloned.1.call-done.rows_ref.refs_1_
  210.1 0.0 copy-start.3
  210.1 1.4 copy-done.3
  211.5 22.5 %shard_map.69 = (f32[2560,512]{1,0:T(8,128)}, bf16[2560,512]{1,0:T(8,128)(2,1)}, bf16[2560,512]{1,0:T(8,128)(2,1)}, f32[2,2560,128]{2,1,0:T(8,128)}) custom-call(s32[1]{0:T(128)} %bitcast.spot_ref, bf16[2560,2048]{1,0:T(8,128)(2,1)} %all-gather.5.cloned.1.call-done.rows_ref.refs_1_, bf16[512,2048]{1,0:T(8,128)(2,1)S(1)} %get-tuple-element.29.head_ref.refs_4_, ...), custom_call_target="tpu_custom_call" | custom-call | flops 13421772800 | bytes 20971520 | tf_op jit(solution)/shard_map/pallas_call | solution.py:153
  234.0 18.5 %all-to-all-done.2 = bf16[4,384,2048]{2,1,0:T(8,128)(2,1)} async-done(((bf16[4,384,2048]{2,1,0:T(8,128)(2,1)}), bf16[4,384,2048]{2,1,0:T(8,128)(2,1)}, u32[]{:S(2)}, u32[]{:S(2)}) %all-to-all-start.2) | async-done | bytes 6291488 | tf_op jit(solution)/shard_map/all_to_all | solution.py:385
  252.5 46.1 %shard_map.70.refs_7_ = f32[2560,2560]{1,0:T(8,128)} custom-call(s32[2]{0:T(128)} %pad_add_fusion.spot_ref, bf16[1536,2048]{1,0:T(8,128)(2,1)} %bitcast.7.refs_0_, bf16[2560,2048]{1,0:T(8,128)(2,1)} %all-gather.5.cloned.1.call-done.rows_ref.refs_1_, bf16[2560,512]{1,0:T(8,128)(2,1)} %get-tuple-element.31.refs_2_, ...), custom_call_target="tpu_custom_call" | custom-call | flops 28185722880 | bytes 26214400 | tf_op jit(solution)/shard_map/pallas_call | solution.py:259
  298.6 0.0 all-gather.3.cloned.1.call-done.refs_0_
  298.6 33.5 %shard_map.71 = f32[2560,2560]{1,0:T(8,128)} custom-call(s32[2]{0:T(128)} %pad_add_fusion.spot_ref, bf16[1024,2048]{1,0:T(8,128)(2,1)} %all-gather.3.cloned.1.call-done.refs_0_, bf16[2560,2048]{1,0:T(8,128)(2,1)} %all-gather.5.cloned.1.call-done.rows_ref.refs_1_, bf16[2560,512]{1,0:T(8,128)(2,1)} %get-tuple-element.31.refs_2_, ...), custom_call_target="tpu_custom_call", output_to_operand_aliasing={{}: (8, {})} | custom-call | flops 18790481920 | bytes 20971520 | tf_op jit(solution)/shard_map/pallas_call | solution.py:259
  (17 shorter events, 0.0 us)
Async XLA Ops:
  7.2 202.9 %all-gather.5.cloned.1.call-start = ((), (), s32[]{:S(2)}) async-start(), calls=%async_computation.4 | async-start | bytes 13107200 | tf_op jit(solution)/shard_map/all_gather | solution.py:369
  7.9 9.8 %copy-start.5 = (bf16[640,2048]{1,0:T(8,128)(2,1)S(1)}, bf16[640,2048]{1,0:T(8,128)(2,1)}, u32[]{:S(2)}) copy-start(bf16[640,2048]{1,0:T(8,128)(2,1)} %param.4) | copy-start | bytes 7864324
  9.6 39.3 %collective-permute-start.5 = (bf16[384,2048]{1,0:T(8,128)(2,1)S(1)}, bf16[384,2048]{1,0:T(8,128)(2,1)S(1)}, u32[]{:S(2)}, u32[]{:S(2)}) collective-permute-start(bf16[384,2048]{1,0:T(8,128)(2,1)S(1)} %slice.30.own), channel_id=1, source_target_pairs={{8,0},{10,2},{12,4},{14,6},{16,8},{18,10},{20,12},{22,14},{24,16},... | collective-permute-start | bytes 4718600 | tf_op jit(solution)/shard_map/ppermute | solution.py:337
  10.9 39.3 %collective-permute-start.3 = (bf16[384,2048]{1,0:T(8,128)(2,1)S(1)}, bf16[384,2048]{1,0:T(8,128)(2,1)}, u32[]{:S(2)}, u32[]{:S(2)}) collective-permute-start(bf16[384,2048]{1,0:T(8,128)(2,1)S(1)} %slice.30.own), channel_id=1, source_target_pairs={{0,8},{2,10},{4,12},{6,14},{8,16},{10,18},{12,20},{14,22},{16,24},... | collective-permute-start | bytes 4718600 | tf_op jit(solution)/shard_map/ppermute | solution.py:337
  18.9 33.2 %collective-permute-start.2 = (bf16[128,2048]{1,0:T(8,128)(2,1)}, bf16[128,2048]{1,0:T(8,128)(2,1)}, u32[]{:S(2)}, u32[]{:S(2)}) collective-permute-start(bf16[128,2048]{1,0:T(8,128)(2,1)} %get-tuple-element.35), channel_id=1, source_target_pairs={{0,6},{1,7}} | collective-permute-start | bytes 1572872 | tf_op jit(solution)/shard_map/ppermute | solution.py:337
  24.4 27.7 %collective-permute-start.1 = (bf16[128,2048]{1,0:T(8,128)(2,1)}, bf16[128,2048]{1,0:T(8,128)(2,1)}, u32[]{:S(2)}, u32[]{:S(2)}) collective-permute-start(bf16[128,2048]{1,0:T(8,128)(2,1)} %get-tuple-element.36), channel_id=1, source_target_pairs={{0,4},{1,5}} | collective-permute-start | bytes 1572872 | tf_op jit(solution)/shard_map/ppermute | solution.py:337
  26.5 42.7 %collective-permute-start = (bf16[128,2048]{1,0:T(8,128)(2,1)}, bf16[128,2048]{1,0:T(8,128)(2,1)}, u32[]{:S(2)}, u32[]{:S(2)}) collective-permute-start(bf16[128,2048]{1,0:T(8,128)(2,1)} %get-tuple-element.37), channel_id=1, source_target_pairs={{0,2},{1,3}} | collective-permute-start | bytes 1572872 | tf_op jit(solution)/shard_map/ppermute | solution.py:337
  49.0 50.6 %collective-permute-start.6 = (bf16[384,2048]{1,0:T(8,128)(2,1)S(1)}, bf16[384,2048]{1,0:T(8,128)(2,1)}, u32[]{:S(2)}, u32[]{:S(2)}) collective-permute-start(bf16[384,2048]{1,0:T(8,128)(2,1)S(1)} %collective-permute-done.5.refs_3_), channel_id=1, source_target_pairs={{8,0},{10,2},{12,4},{14,6},{16,8},{18,10},{20,12},{22,14},{9,1},{1... | collective-permute-start | bytes 4718600 | tf_op jit(solution)/shard_map/ppermute | solution.py:337
  50.3 49.9 %collective-permute-start.4 = (bf16[384,2048]{1,0:T(8,128)(2,1)}, bf16[384,2048]{1,0:T(8,128)(2,1)}, u32[]{:S(2)}, u32[]{:S(2)}) collective-permute-start(bf16[384,2048]{1,0:T(8,128)(2,1)} %collective-permute-done.3.refs_0_), channel_id=1, source_target_pairs={{8,16},{10,18},{12,20},{14,22},{16,24},{18,26},{20,28},{22,30},{9,... | collective-permute-start | bytes 4718600 | tf_op jit(solution)/shard_map/ppermute | solution.py:337
  71.3 38.7 %all-to-all-start = ((bf16[4,64,2048]{2,1,0:T(8,128)(2,1)}), bf16[4,64,2048]{2,1,0:T(8,128)(2,1)}, u32[]{:S(2)}, u32[]{:S(2)}) async-start(bf16[4,64,2048]{2,1,0:T(8,128)(2,1)} %bitcast.13), calls=%async_computation | async-start | bytes 2097152 | tf_op jit(solution)/shard_map/all_to_all | solution.py:372
  76.6 20.1 %collective-permute-start.9 = (s16[512,128]{1,0:T(8,128)(2,1)S(1)}, s16[512,128]{1,0:T(8,128)(2,1)S(1)}, u32[]{:S(2)}, u32[]{:S(2)}) collective-permute-start(s16[512,128]{1,0:T(8,128)(2,1)S(1)} %slice_convert_fusion), channel_id=1, source_target_pairs={{0,24},{2,26},{4,28},{6,30},{1,25},{3,27},{5,29},{7,31}} | collective-permute-start | bytes 393224 | tf_op jit(solution)/shard_map/ppermute | solution.py:337
  82.3 15.9 %collective-permute-start.8 = (s16[512,128]{1,0:T(8,128)(2,1)S(1)}, s16[512,128]{1,0:T(8,128)(2,1)S(1)}, u32[]{:S(2)}, u32[]{:S(2)}) collective-permute-start(s16[512,128]{1,0:T(8,128)(2,1)S(1)} %slice_convert_fusion), channel_id=1, source_target_pairs={{0,16},{2,18},{4,20},{6,22},{1,17},{3,19},{5,21},{7,23}} | collective-permute-start | bytes 393224 | tf_op jit(solution)/shard_map/ppermute | solution.py:337
  83.6 16.0 %collective-permute-start.7 = (s16[512,128]{1,0:T(8,128)(2,1)S(1)}, s16[512,128]{1,0:T(8,128)(2,1)S(1)}, u32[]{:S(2)}, u32[]{:S(2)}) collective-permute-start(s16[512,128]{1,0:T(8,128)(2,1)S(1)} %slice_convert_fusion), channel_id=1, source_target_pairs={{0,8},{2,10},{4,12},{6,14},{1,9},{3,11},{5,13},{7,15}} | collective-permute-start | bytes 393224 | tf_op jit(solution)/shard_map/ppermute | solution.py:337
  99.5 0.6 copy-start.6
  100.2 61.6 %collective-permute-start.13 = (bf16[384,2048]{1,0:T(8,128)(2,1)}, bf16[384,2048]{1,0:T(8,128)(2,1)}, u32[]{:S(2)}, u32[]{:S(2)}) collective-permute-start(bf16[384,2048]{1,0:T(8,128)(2,1)} %collective-permute-done.4.refs_1_), channel_id=1, source_target_pairs={{16,24},{18,26},{20,28},{22,30},{17,25},{19,27},{21,29},{23,31}} | collective-permute-start | bytes 4718600 | tf_op jit(solution)/shard_map/ppermute | solution.py:337
  102.0 59.8 %collective-permute-start.14 = (bf16[384,2048]{1,0:T(8,128)(2,1)}, bf16[384,2048]{1,0:T(8,128)(2,1)}, u32[]{:S(2)}, u32[]{:S(2)}) collective-permute-start(bf16[384,2048]{1,0:T(8,128)(2,1)} %collective-permute-done.6.refs_4_), channel_id=1, source_target_pairs={{8,0},{10,2},{12,4},{14,6},{9,1},{11,3},{13,5},{15,7}} | collective-permute-start | bytes 4718600 | tf_op jit(solution)/shard_map/ppermute | solution.py:337
  110.0 51.8 %all-to-all-start.1 = ((bf16[4,64,2048]{2,1,0:T(8,128)(2,1)}), bf16[4,64,2048]{2,1,0:T(8,128)(2,1)}, u32[]{:S(2)}, u32[]{:S(2)}) async-start(bf16[4,64,2048]{2,1,0:T(8,128)(2,1)} %all-to-all-done), calls=%async_computation.1 | async-start | bytes 2097152 | tf_op jit(solution)/shard_map/all_to_all | solution.py:378
  114.3 184.3 %all-gather.3.cloned.1.call-start = ((), (), s32[]{:S(2)}) async-start(), calls=%async_computation.3 | async-start | bytes 5242880 | tf_op jit(solution)/shard_map/all_gather | solution.py:386
  114.3 26.6 %collective-permute-start.12 = (bf16[128,2048]{1,0:T(8,128)(2,1)}, bf16[128,2048]{1,0:T(8,128)(2,1)}, u32[]{:S(2)}, u32[]{:S(2)}) collective-permute-start(bf16[128,2048]{1,0:T(8,128)(2,1)} %select_select_fusion.1), channel_id=1, source_target_pairs={{0,24},{2,26},{4,28},{6,30},{1,25},{3,27},{5,29},{7,31}} | collective-permute-start | bytes 1572872 | tf_op jit(solution)/shard_map/ppermute | solution.py:337
  128.6 23.1 %collective-permute-start.11 = (bf16[128,2048]{1,0:T(8,128)(2,1)}, bf16[128,2048]{1,0:T(8,128)(2,1)}, u32[]{:S(2)}, u32[]{:S(2)}) collective-permute-start(bf16[128,2048]{1,0:T(8,128)(2,1)} %select_select_fusion.1), channel_id=1, source_target_pairs={{0,16},{2,18},{4,20},{6,22},{1,17},{3,19},{5,21},{7,23}} | collective-permute-start | bytes 1572872 | tf_op jit(solution)/shard_map/ppermute | solution.py:337
  130.7 29.1 %collective-permute-start.10 = (bf16[128,2048]{1,0:T(8,128)(2,1)}, bf16[128,2048]{1,0:T(8,128)(2,1)}, u32[]{:S(2)}, u32[]{:S(2)}) collective-permute-start(bf16[128,2048]{1,0:T(8,128)(2,1)} %select_select_fusion.1), channel_id=1, source_target_pairs={{0,8},{2,10},{4,12},{6,14},{1,9},{3,11},{5,13},{7,15}} | collective-permute-start | bytes 1572872 | tf_op jit(solution)/shard_map/ppermute | solution.py:337
  161.8 22.2 %collective-permute-start.17 = (bf16[128,2048]{1,0:T(8,128)(2,1)}, bf16[128,2048]{1,0:T(8,128)(2,1)}, u32[]{:S(2)}, u32[]{:S(2)}) collective-permute-start(bf16[128,2048]{1,0:T(8,128)(2,1)} %select_select_fusion.refs_0_), channel_id=1, source_target_pairs={{0,6},{2,4},{4,2},{6,0},{8,14},{10,12},{12,10},{14,8},{16,22},{18,... | collective-permute-start | bytes 1572872 | tf_op jit(solution)/shard_map/ppermute | solution.py:337
  164.4 22.1 %collective-permute-start.16 = (bf16[128,2048]{1,0:T(8,128)(2,1)}, bf16[128,2048]{1,0:T(8,128)(2,1)}, u32[]{:S(2)}, u32[]{:S(2)}) collective-permute-start(bf16[128,2048]{1,0:T(8,128)(2,1)} %select_select_fusion.refs_0_), channel_id=1, source_target_pairs={{0,4},{2,6},{4,0},{6,2},{8,12},{10,14},{12,8},{14,10},{16,20},{18,... | collective-permute-start | bytes 1572872 | tf_op jit(solution)/shard_map/ppermute | solution.py:337
  165.0 22.3 %collective-permute-start.15 = (bf16[128,2048]{1,0:T(8,128)(2,1)}, bf16[128,2048]{1,0:T(8,128)(2,1)}, u32[]{:S(2)}, u32[]{:S(2)}) collective-permute-start(bf16[128,2048]{1,0:T(8,128)(2,1)} %select_select_fusion.refs_0_), channel_id=1, source_target_pairs={{0,2},{2,0},{4,6},{6,4},{8,10},{10,8},{12,14},{14,12},{16,18},{18,... | collective-permute-start | bytes 1572872 | tf_op jit(solution)/shard_map/ppermute | solution.py:337
  175.7 2.7 copy-start
  178.5 74.0 %all-to-all-start.2 = ((bf16[4,384,2048]{2,1,0:T(8,128)(2,1)}), bf16[4,384,2048]{2,1,0:T(8,128)(2,1)}, u32[]{:S(2)}, u32[]{:S(2)}) async-start(bf16[4,384,2048]{2,1,0:T(8,128)(2,1)} %bitcast.10), calls=%async_computation.2 | async-start | bytes 12582912 | tf_op jit(solution)/shard_map/all_to_all | solution.py:385
  187.3 1.0 copy-start.4
  210.0 24.0 %copy-start.1 = (bf16[512,2048]{1,0:T(8,128)(2,1)}, bf16[512,2048]{1,0:T(8,128)(2,1)S(1)}, u32[]{:S(2)}) copy-start(bf16[512,2048]{1,0:T(8,128)(2,1)S(1)} %get-tuple-element.29.head_ref.refs_4_) | copy-start | bytes 6291460
  210.0 24.0 %copy-start.2 = (f32[512,512]{1,0:T(8,128)}, f32[512,512]{1,0:T(8,128)S(1)}, u32[]{:S(2)}) copy-start(f32[512,512]{1,0:T(8,128)S(1)} %get-tuple-element.30.inv_ref.refs_5_) | copy-start | bytes 3145732
  210.1 1.4 copy-start.3
Sparse Core Ops, SparseCore 0:
  9.8 137.0 all-gather.4
  173.6 81.8 all-gather.2
